TPU v7x, 128 devices: a whole 4x4x4 slice. The times are simulated.
128 devices in a mesh: gx: 8 (over y, core), gy: 16 (over z, x).
Axes of the slice: x: 4, y: 4, z: 4, core: 2. Of those that a mesh axis runs over, the one named last changes fastest.
Arguments:
- nest_fields: bfloat16 [5, 16, 2048, 2048], P(None, None, 'gy', 'gx'), may hold values from -4 to 4, as said below
- parent_modes: float32 [5, 16, 64, 64], replicated, may hold values from -0.2 to 0.2
- nest_offset: int32 [2], replicated, may hold values from 0 to 2047
- level_mask: int32 [16], replicated, may hold values 0 or 1
- strength: float32 [5], replicated, may hold values from 0.2 to 1
Outputs:
- nudged: bfloat16 [5, 16, 2048, 2048], P(None, None, 'gy', 'gx')
Inputs may be any that keep to these rules, and one draw needn't show every extreme that they name: `nest_fields`: nest fields hold large-scale waves of every field and level beside small-scale noise.
All inputs are finite; a program needn't handle non-finite values.
Results may differ from a plain program's by a relative error of at most 0.0012.
Values sent between devices are 32-bit elements; how exact they have to be, the bound alone decides.
No kernel may reach another device: no remote copies, remote signals or barrier semaphores. Data moves between devices by JAX's collectives and lax.ppermute only.
A program may use at most 64 MiB of HBM per device.

v0:
```python
import math

import jax
import jax.numpy as jnp
from jax import lax
from jax.sharding import PartitionSpec as P


def wave_table(mode_count, full_length, first_cell, cell_count, cell_shift):
    positions = (first_cell + jnp.arange(cell_count, dtype=jnp.int32) + cell_shift) % full_length
    half_count = mode_count // 2
    wavenumbers = jnp.concatenate(
        [jnp.arange(half_count, dtype=jnp.int32), jnp.arange(1, half_count + 1, dtype=jnp.int32)]
    )
    phase_int = wavenumbers[:, None] * positions[None, :] % full_length
    angles = 2.0 * math.pi / full_length * phase_int.astype(jnp.float32)
    is_cosine = jnp.arange(mode_count, dtype=jnp.int32)[:, None] < half_count
    return jnp.where(is_cosine, jnp.cos(angles), jnp.sin(angles))


def per_device(nest_fields, parent_modes, nest_offset, level_mask, strength):
    highest = lax.Precision.HIGHEST
    field_count, level_count, row_count, col_count = nest_fields.shape
    mode_count = parent_modes.shape[-1]
    width_x = col_count * lax.axis_size("gx")
    width_y = row_count * lax.axis_size("gy")
    first_x = lax.axis_index("gx") * col_count
    first_y = lax.axis_index("gy") * row_count
    zero_shift = jnp.zeros((), jnp.int32)
    table_x = wave_table(mode_count, width_x, first_x, col_count, zero_shift)
    table_y = wave_table(mode_count, width_y, first_y, row_count, zero_shift)
    shift_x = wave_table(mode_count, width_x, first_x, col_count, nest_offset[0])
    shift_y = wave_table(mode_count, width_y, first_y, row_count, nest_offset[1])
    rounded_x = table_x.astype(jnp.bfloat16)
    along_x = jnp.einsum(
        "flyx,ax->flya", nest_fields, rounded_x, preferred_element_type=jnp.float32
    )
    partial_sums = jnp.einsum("by,flya->flba", table_y, along_x, precision=highest)
    mode_sums = lax.psum(partial_sums, ("gx", "gy"))
    weights = jnp.where(jnp.arange(mode_count) == 0, 1.0, 2.0).astype(jnp.float32)
    nest_modes = mode_sums * (weights[:, None] * weights[None, :] / (width_x * width_y))
    parent_cols = jnp.einsum("flba,ax->flbx", parent_modes, shift_x, precision=highest)
    nest_cols = jnp.einsum("flba,ax->flbx", nest_modes, table_x, precision=highest)
    stacked = jnp.concatenate([parent_cols, -nest_cols], axis=2)
    row_tables = jnp.concatenate([shift_y, table_y], axis=0)
    correction = jnp.einsum("flkx,ky->flyx", stacked, row_tables, precision=highest)
    blend_gain = strength[:, None] * level_mask[None, :].astype(jnp.float32)
    return (nest_fields.astype(jnp.float32) + blend_gain[:, :, None, None] * correction).astype(
        jnp.bfloat16
    )


def solution(mesh):
    in_specs = (P(None, None, "gy", "gx"), P(), P(), P(), P())
    out_specs = P(None, None, "gy", "gx")
    return jax.shard_map(
        per_device, mesh=mesh, in_specs=in_specs, out_specs=out_specs, check_vma=False
    )
```

profile of v0, /device:TPU:1, one launch (start us, length us, event | category | flops | bytes accessed | tf_op | source)
XLA Modules:
  0.0 197.6 jit_solution(4864387715978326453)
XLA Ops:
  6.5 0.0 copy-start
  6.5 0.0 all-reduce.2.cloned.1.call-start
  6.6 0.1 pad_add_fusion
  6.7 4.6 %fusion.42 = f32[64,5,16,128]{3,0,2,1:T(8,128)S(1)} fusion(bf16[5,16,128,256]{3,2,1,0:T(8,128)(2,1)} %param.5, s32[256]{0:T(256)S(1)} %and_select_fusion, s32[64]{0:T(128)S(1)} %pad_add_fusion, pred[64]{0:T(512)(128)(4,1)S(1)} %iota_compare_fusion), kind=kOutput, calls=%fused_computation.61 | convolution fusion | flops 335806464 | bytes 7865664 | tf_op jit(solution)/shard_map/flyx,ax->flya/dot_general | solution.py:35
  11.3 0.0 copy-start.4
  11.3 0.0 copy-start.2
  11.3 0.0 copy-start.3
  11.3 4.0 %fusion.14 = f32[5,16,64,64]{2,3,1,0:T(8,128)} fusion(f32[64,5,16,128]{3,0,2,1:T(8,128)S(1)} %fusion.42, s32[128]{0:T(128)S(1)} %and_select_fusion.2, s32[64]{0:T(128)S(1)} %pad_add_fusion, pred[64]{0:T(512)(128)(4,1)S(1)} %iota_compare_fusion), kind=kOutput, calls=%fused_computation.12 | convolution fusion | flops 503439360 | bytes 3932992 | tf_op jit(solution)/shard_map/by,flya->flba/dot_general | solution.py:38
  15.3 0.0 all-reduce.2.cloned.1.call-update
  15.3 0.0 copy-done.4
  15.4 0.0 copy-done.2
  15.4 0.6 fusion.73
  16.0 0.6 and_select_fusion.1
  16.5 0.1 multiply_multiply_fusion
  16.6 0.0 copy-done.3
  16.6 0.1 broadcast_multiply_fusion
  16.7 0.7 and_select_fusion.3
  17.4 0.6 sine_select_fusion.2
  18.0 0.0 copy-done
  18.0 6.7 %convolution_bitcast_fusion = f32[5,16,64,256]{3,2,1,0:T(8,128)} fusion(f32[5,16,64,64]{3,2,1,0:T(8,128)S(1)} %copy-done, s32[256]{0:T(256)S(1)} %and_select_fusion.1, s32[64]{0:T(128)S(1)} %pad_add_fusion, pred[64]{0:T(512)(128)(4,1)S(1)} %iota_compare_fusion), kind=kOutput, calls=%fused_computation.11 | convolution fusion | flops 1006878720 | bytes 6554944 | tf_op jit(solution)/shard_map/flba,ax->flbx/dot_general | solution.py:42
  24.7 145.8 %all-reduce.2.cloned.1.call-done = f32[5,16,64,64]{2,3,1,0:T(8,128)} async-done(((f32[5,16,64,64]{2,3,1,0:T(8,128)}), f32[5,16,64,64]{2,3,1,0:T(8,128)}) %all-reduce.2.cloned.1.call-update) | async-done | bytes 1310736 | tf_op jit(solution)/shard_map/psum | solution.py:39
  170.5 0.0 copy-start.1
  170.5 6.6 %fusion.11 = f32[5,16,64,256]{3,2,1,0:T(8,128)S(1)} fusion(f32[5,16,64,64]{2,3,1,0:T(8,128)} %all-reduce.2.cloned.1.call-done, f32[64,64]{0,1:T(8,128)S(1)} %multiply_multiply_fusion, s32[256]{0:T(256)S(1)} %and_select_fusion, s32[64]{0:T(128)S(1)} %pad_add_fusion, pred[64]{0:T(512)(128)(4,1)S(1)} %iota_compare_fusion), kind=kOutput, calls=%fused_computation.10 | convolution fusion | flops 1008517120 | bytes 6571328 | tf_op jit(solution)/shard_map/flba,ax->flbx/dot_general | solution.py:43
  177.2 0.0 copy-done.1
  177.2 13.6 %fusion.4 = bf16[5,16,128,256]{3,2,1,0:T(8,128)(2,1)} fusion(bf16[5,16,128,256]{3,2,1,0:T(8,128)(2,1)} %param.5, f32[5,16]{1,0:T(8,128)S(1)} %broadcast_multiply_fusion, f32[5,16,64,256]{3,2,1,0:T(8,128)S(1)} %fusion.11, f32[5,16,64,256]{3,2,1,0:T(8,128)S(1)} %copy-done.1, f32[64,128]{0,1:T(8,128)S(1)} %get-tuple-element.6, f32[64,128]{0,1:T(8,128)S(1)} %get-tuple-element.5), kind=kOutput, calls=%fused_computation.5 | convolution fusion | flops 4039655424 | bytes 21037376 | tf_op jit(solution)/shard_map/flkx,ky->flyx/dot_general | solution.py:46
  (7 shorter events, 0.0 us)
Async XLA Ops:
  6.5 11.4 %copy-start = (f32[5,16,64,64]{3,2,1,0:T(8,128)S(1)}, f32[5,16,64,64]{3,2,1,0:T(8,128)}, u32[]{:S(2)}) copy-start(f32[5,16,64,64]{3,2,1,0:T(8,128)} %param.6) | copy-start | bytes 3932164
  6.5 164.0 %all-reduce.2.cloned.1.call-start = ((), (), s32[]{:S(2)}) async-start(), calls=%async_computation | async-start | bytes 5242880 | tf_op jit(solution)/shard_map/psum | solution.py:39
  11.3 4.1 %copy-start.4 = (s32[16]{0:T(128)S(1)}, s32[16]{0:T(128)}, u32[]{:S(2)}) copy-start(s32[16]{0:T(128)} %param.8) | copy-start | bytes 196
  11.3 4.1 %copy-start.2 = (s32[2]{0:T(128)S(1)}, s32[2]{0:T(128)}, u32[]{:S(2)}) copy-start(s32[2]{0:T(128)} %param.7) | copy-start | bytes 28
  11.3 5.3 %copy-start.3 = (f32[5]{0:T(128)S(1)}, f32[5]{0:T(128)}, u32[]{:S(2)}) copy-start(f32[5]{0:T(128)} %param.9) | copy-start | bytes 64
  170.5 6.6 %copy-start.1 = (f32[5,16,64,256]{3,2,1,0:T(8,128)S(1)}, f32[5,16,64,256]{3,2,1,0:T(8,128)}, u32[]{:S(2)}) copy-start(f32[5,16,64,256]{3,2,1,0:T(8,128)} %convolution_bitcast_fusion) | copy-start | bytes 15728644
Sparse Core Ops, SparseCore 0:
  15.5 155.0 all-reduce.1
where the time goes:
time: 198 us
  waiting for transfers between devices  146 us (74%)
  matrix products  35.5 us (18%)
  between operations  13.5 us (7%)
  other arithmetic  2.09 us (1%)
    psum x1, waiting for transfers between devices, per_device(): mode_sums = lax.psum(partial_sums, ('gx', 'gy'))  146 us
    dot_general x1, matrix products, per_device(): jnp.einsum('flkx,ky->flyx', stacked, row_tables, precision=highest)  13.6 us
    dot_general x1, matrix products, per_device(): jnp.einsum('flba,ax->flbx', parent_modes, shift_x, precision=highest)  6.74 us
    dot_general x1, matrix products, per_device(): jnp.einsum('flba,ax->flbx', nest_modes, table_x, precision=highest)  6.6 us
    dot_general x1, matrix products, per_device(): jnp.einsum('flyx,ax->flya', nest_fields, rounded_x, preferred_element_typ...  4.56 us
    dot_general x1, matrix products, per_device(): jnp.einsum('by,flya->flba', table_y, along_x, precision=highest)  4.02 us
  transfers between devices with their start and end apart: 1, of which 1 were waited for; matrix products, arithmetic and copies ran while one was open for 5% of the time, Pallas kernels for 0%

commit v1 on v0

v1 whole, which is shorter than its diff:
```python
import functools
import math

import jax
import jax.numpy as jnp
import numpy as np
from jax import lax
from jax.experimental import pallas as pl
from jax.experimental.pallas import tpu as pltpu
from jax.sharding import PartitionSpec as P

MODES = 64
HALF = MODES // 2
CELLS = 2048
ROWS = 128
COLS = 256
SLABS = 80
LEVELS = 16
PAIRS = SLABS // 2
HALF_PAIRS = PAIRS // 2
F32 = jnp.float32
BF16 = jnp.bfloat16
VMEM_LIMIT = 48 * 1024 * 1024


def split_bf16(value):
    high = value.astype(BF16)
    low = (value - high.astype(F32)).astype(BF16)
    return high, low


def numpy_table():
    wave = np.concatenate([np.arange(HALF), np.arange(1, HALF + 1)])
    phase = (wave[:, None] * np.arange(CELLS)[None, :]) % CELLS
    angle = phase * (2.0 * math.pi / CELLS)
    cosine = np.arange(MODES)[:, None] < HALF
    return np.where(cosine, np.cos(angle), np.sin(angle)).astype(np.float32)


def forward_constants():
    table = numpy_table()
    rounded = table.astype(BF16)
    columns = np.concatenate([rounded.T, rounded.T], axis=1)
    high = rounded
    low = (table - high.astype(np.float32)).astype(BF16)
    tiles = CELLS // ROWS
    high = high.reshape(MODES, tiles, ROWS).transpose(1, 0, 2)
    low = low.reshape(MODES, tiles, ROWS).transpose(1, 0, 2)
    rows = np.concatenate([high, high, low], axis=2)
    return columns, rows


def forward_kernel(place_ref, field_ref, cols_ref, rows_ref, out_ref, weight_ref):
    @pl.when(pl.program_id(0) == 0)
    def _():
        table = cols_ref[...]
        lane = lax.broadcasted_iota(jnp.int32, table.shape, 1)
        zero = jnp.zeros_like(table)
        weight_ref[0:COLS, :] = jnp.where(lane < MODES, table, zero)
        weight_ref[COLS:, :] = jnp.where(lane < MODES, zero, table)

    pairs = field_ref.shape[0]
    left = field_ref[:, 0].reshape(pairs * ROWS, COLS)
    right = field_ref[:, 1].reshape(pairs * ROWS, COLS)
    along = jnp.dot(left, weight_ref[0:COLS, :], preferred_element_type=F32)
    along += jnp.dot(right, weight_ref[COLS:, :], preferred_element_type=F32)
    table_y = rows_ref[0]
    for quad in range(pairs // 2):
        first = along[(2 * quad) * ROWS : (2 * quad + 1) * ROWS]
        second = along[(2 * quad + 1) * ROWS : (2 * quad + 2) * ROWS]
        high, low = split_bf16(jnp.concatenate([first, second], axis=1))
        stacked = jnp.concatenate([high, low, high], axis=0)
        sums = jnp.dot(table_y, stacked, preferred_element_type=F32)
        out_ref[2 * quad] = sums[:, 0:128]
        out_ref[2 * quad + 1] = sums[:, 128:256]


def forward(place, field, columns, rows, steps):
    block = HALF_PAIRS // steps
    return pl.pallas_call(
        forward_kernel,
        grid_spec=pltpu.PrefetchScalarGridSpec(
            num_scalar_prefetch=1,
            grid=(steps,),
            in_specs=[
                pl.BlockSpec((block, 2, ROWS, COLS), lambda i, s: (s[0] * steps + i, 0, 0, 0)),
                pl.BlockSpec((COLS, 128), lambda i, s: (s[1], 0)),
                pl.BlockSpec((1, MODES, 3 * ROWS), lambda i, s: (s[2], 0, 0)),
            ],
            out_specs=pl.BlockSpec((block, MODES, 128), lambda i, s: (i, 0, 0)),
            scratch_shapes=[pltpu.VMEM((2 * COLS, 128), BF16)],
        ),
        out_shape=jax.ShapeDtypeStruct((HALF_PAIRS, MODES, 128), F32),
        compiler_params=pltpu.CompilerParams(vmem_limit_bytes=VMEM_LIMIT),
        cost_estimate=pl.CostEstimate(
            flops=2 * HALF_PAIRS * 2 * ROWS * COLS * MODES,
            bytes_accessed=HALF_PAIRS * 2 * ROWS * COLS * 2 + HALF_PAIRS * MODES * 128 * 4,
            transcendentals=0,
        ),
        name="forward_modes",
    )(place, field, columns, rows)


def wave_sine(wave, cosine, position):
    phase = wave * position + jnp.where(cosine, CELLS // 4, 0)
    phase = ((phase + CELLS // 2) & (CELLS - 1)) - CELLS // 2
    return jnp.sin(phase.astype(F32) * (2.0 * math.pi / CELLS))


def tables_kernel(place_ref, offset_ref, rows_ref, even_ref, odd_ref):
    first_x = place_ref[1] * COLS
    first_y = place_ref[2] * ROWS
    shift_x = offset_ref[0]
    shift_y = offset_ref[1]
    mode = lax.broadcasted_iota(jnp.int32, (ROWS, 128), 1)
    position = lax.broadcasted_iota(jnp.int32, (ROWS, 128), 0) + first_y
    shifted = mode >= MODES
    mode = mode & (MODES - 1)
    wave = jnp.where(mode < HALF, mode, mode - (HALF - 1))
    position = position + jnp.where(shifted, shift_y, 0)
    value = wave_sine(wave, mode < HALF, position)
    value = jnp.where(shifted | (mode == 0), value, 2.0 * value)
    high, low = split_bf16(value)
    for part in range(2):
        lanes = slice(part * MODES, (part + 1) * MODES)
        rows_ref[part] = jnp.concatenate([high[:, lanes], high[:, lanes], low[:, lanes]], axis=1)
    mode = lax.broadcasted_iota(jnp.int32, (MODES, COLS), 0)
    wave = jnp.where(mode < HALF, mode, mode - (HALF - 1))
    position = lax.broadcasted_iota(jnp.int32, (MODES, COLS), 1) + first_x
    nest = wave_sine(wave, mode < HALF, position)
    scale = 1.0 / (CELLS * CELLS)
    nest = nest * jnp.where(mode == 0, -scale, -2.0 * scale)
    parent = wave_sine(wave, mode < HALF, position + shift_x)
    nest_high, nest_low = split_bf16(nest)
    parent_high, parent_low = split_bf16(parent)
    even_ref[...] = jnp.concatenate(
        [nest_high, parent_high, nest_high, parent_high, nest_low, parent_low], axis=0
    )
    odd_ref[...] = jnp.concatenate(
        [parent_high, nest_high, parent_high, nest_high, parent_low, nest_low], axis=0
    )


def inverse_tables(place, offset):
    smem = pl.BlockSpec(memory_space=pltpu.SMEM)
    return pl.pallas_call(
        tables_kernel,
        in_specs=[smem, smem],
        out_shape=[
            jax.ShapeDtypeStruct((2, ROWS, 3 * MODES), BF16),
            jax.ShapeDtypeStruct((6 * MODES, COLS), BF16),
            jax.ShapeDtypeStruct((6 * MODES, COLS), BF16),
        ],
        name="inverse_tables",
    )(place, offset)


def inverse_kernel(
    side, steps, place_ref, mask_ref, gain_ref, field_ref, modes_ref, parent_ref, rows_ref, even_ref, odd_ref, *rest
):
    out_ref = rest[-1]
    pairs = field_ref.shape[0]
    core = place_ref[0]
    half = core if side == 0 else 1 - core
    first_pair = half * HALF_PAIRS + pl.program_id(0) * pairs
    lane = lax.broadcasted_iota(jnp.int32, (1, 128), 1)
    is_left = lane < MODES
    left = lax.broadcasted_iota(jnp.int32, (ROWS, 128), 1) < MODES

    def gain(pair, slot):
        slab = 2 * (first_pair + pair) + slot
        field = slab // LEVELS
        level = slab - field * LEVELS
        return gain_ref[field] * mask_ref[level].astype(F32)

    def along_rows(part, first, second):
        high, low = split_bf16(jnp.concatenate([first, second], axis=1))
        stacked = jnp.concatenate([high, low, high], axis=0)
        return jnp.dot(rows_ref[part], stacked, preferred_element_type=F32)

    even, odd = [], []
    for quad in range(pairs // 2):
        nest, parent = [], []
        for pair in (2 * quad, 2 * quad + 1):
            gain_left, gain_right = gain(pair, 0), gain(pair, 1)
            nest.append(modes_ref[pair] * jnp.where(is_left, gain_left, gain_right))
            both = jnp.concatenate([parent_ref[pair, 1], parent_ref[pair, 0]], axis=1)
            parent.append(both * jnp.where(is_left, gain_right, gain_left))
        nest_high, nest_low = split_bf16(along_rows(0, *nest))
        parent_high, parent_low = split_bf16(along_rows(1, *parent))
        for slot in range(2):
            lanes = slice(slot * 128, (slot + 1) * 128)
            nh, nl = nest_high[:, lanes], nest_low[:, lanes]
            ph, pw = parent_high[:, lanes], parent_low[:, lanes]
            high = jnp.where(left, nh, ph)
            even.append(jnp.concatenate([high, jnp.where(left, nl, pw), high], axis=1))
            high = jnp.where(left, ph, nh)
            odd.append(jnp.concatenate([high, jnp.where(left, pw, nl), high], axis=1))
    for slot, (rows, table) in enumerate(((even, even_ref), (odd, odd_ref))):
        correction = jnp.dot(jnp.concatenate(rows, axis=0), table[...], preferred_element_type=F32)
        correction = correction.reshape(pairs, ROWS, COLS)
        out_ref[:, slot] = (field_ref[:, slot].astype(F32) + correction).astype(BF16)


def inverse(side, steps, place, mask, strength, field, modes, parent, tables, previous):
    block = HALF_PAIRS // steps
    smem = pl.BlockSpec(memory_space=pltpu.SMEM)

    def here(i, s):
        half = s[0] if side == 0 else 1 - s[0]
        return (half * steps + i, 0, 0, 0)

    in_specs = [
        smem,
        smem,
        pl.BlockSpec((block, 2, ROWS, COLS), here),
        pl.BlockSpec((block, MODES, 128), lambda i, s: (i, 0, 0)),
        pl.BlockSpec((block, 2, MODES, MODES), here),
        pl.BlockSpec((2, ROWS, 3 * MODES), lambda i, s: (0, 0, 0)),
        pl.BlockSpec((6 * MODES, COLS), lambda i, s: (0, 0)),
        pl.BlockSpec((6 * MODES, COLS), lambda i, s: (0, 0)),
    ]
    operands = [mask, strength, field, modes, parent, *tables]
    aliases = {}
    if previous is not None:
        in_specs.append(pl.BlockSpec(memory_space=pl.ANY))
        operands.append(previous)
        aliases = {len(operands): 0}
    return pl.pallas_call(
        functools.partial(inverse_kernel, side, steps),
        grid_spec=pltpu.PrefetchScalarGridSpec(
            num_scalar_prefetch=1,
            grid=(steps,),
            in_specs=in_specs,
            out_specs=pl.BlockSpec((block, 2, ROWS, COLS), here),
        ),
        out_shape=jax.ShapeDtypeStruct((PAIRS, 2, ROWS, COLS), BF16),
        input_output_aliases=aliases,
        compiler_params=pltpu.CompilerParams(vmem_limit_bytes=VMEM_LIMIT),
        cost_estimate=pl.CostEstimate(
            flops=2 * HALF_PAIRS * 2 * ROWS * COLS * 6 * MODES,
            bytes_accessed=HALF_PAIRS * 2 * ROWS * COLS * 4 + HALF_PAIRS * MODES * 128 * 4,
            transcendentals=0,
        ),
        name="inverse_own" if side == 0 else "inverse_other",
    )(place, *operands)


def device_index(y, core, row):
    return (2 * y + core) * 16 + row


def reduce_groups():
    return [
        [device_index(y, core, row) for y in pair for row in range(16)]
        for core in range(2)
        for pair in ((0, 1), (3, 2))
    ]


CORE_SWAP = [(i, i ^ 1) for i in range(8)]
Y_SWAP = [(2 * y + c, 2 * (3 - y) + c) for y in range(4) for c in range(2)]


def per_device(nest_fields, parent_modes, nest_offset, level_mask, strength):
    index_x = lax.axis_index("gx")
    index_y = lax.axis_index("gy")
    core = index_x & 1
    place = jnp.stack([core, index_x, index_y]).astype(jnp.int32)
    other = jnp.stack([1 - core, index_x, index_y]).astype(jnp.int32)
    field = nest_fields.reshape(PAIRS, 2, ROWS, COLS)
    parent = parent_modes.reshape(PAIRS, 2, MODES, MODES)
    columns, rows = forward_constants()
    columns, rows = jnp.asarray(columns), jnp.asarray(rows)
    groups = reduce_groups()
    members = len(groups[0])

    for_partner = forward(other, field, columns, rows, 2)
    from_partner = lax.ppermute(for_partner, "gx", CORE_SWAP)
    own = forward(place, field, columns, rows, 2)
    own = (own + from_partner).reshape(members, -1, 128)

    def exchange(pieces):
        return lax.all_to_all(pieces, ("gx", "gy"), 0, 0, axis_index_groups=groups, tiled=True)

    piece = exchange(own).sum(0)
    piece = piece + lax.ppermute(piece, "gx", Y_SWAP)
    tables = inverse_tables(place, nest_offset)
    sums = exchange(jnp.broadcast_to(piece[None], (members,) + piece.shape))
    sums = sums.reshape(HALF_PAIRS, MODES, 128)
    other_sums = lax.ppermute(sums, "gx", CORE_SWAP)
    out = inverse(0, 2, place, level_mask, strength, field, sums, parent, tables, None)
    out = inverse(1, 2, place, level_mask, strength, field, other_sums, parent, tables, out)
    return out.reshape(nest_fields.shape)


def solution(mesh):
    in_specs = (P(None, None, "gy", "gx"), P(), P(), P(), P())
    out_specs = P(None, None, "gy", "gx")
    return jax.shard_map(
        per_device, mesh=mesh, in_specs=in_specs, out_specs=out_specs, check_vma=False
    )
```

time: 198 us -> 70.3 us (0.36)
  waiting for transfers between devices: 146 us -> 1.95 us
  matrix products: 35.5 us -> 0 us
  blocking collectives: 0 us -> 34.5 us
  Pallas kernels: 0 us -> 19.9 us
  between operations: 13.5 us -> 0.09 us
  starting transfers between devices: 0.01 us -> 7.58 us
  local copies, waits for them, and re-layouts: 0.61 us -> 5.63 us
    psum x1 -> x0, waiting for transfers between devices: 146 us -> none  [per_device(): mode_sums = lax.psum(partial_sums, ('gx', 'gy'))]
    dot_general x5 -> x0, matrix products: 35.5 us -> none  [the longest x1 13.6 us: per_device(): jnp.einsum('flkx,ky->flyx', stacked, row_tables, precision=highest)]
    all_to_all x0 -> x2, blocking collectives: none -> 34.5 us  [exchange(): lax.all_to_all(pieces, ('gx', 'gy'), 0, 0, axis_index_groups=groups, tile...]
    pallas_call x0 -> x5, Pallas kernels: none -> 19.9 us  [the longest x2 10.4 us: inverse(): pl.pallas_call(functools.partial(inverse_kernel, side, steps), grid_spec=...]
    ppermute x0 -> x3, starting transfers between devices: none -> 7.58 us  [the longest x1 4.1 us: per_device(): other_sums = lax.ppermute(sums, 'gx', CORE_SWAP)]
    unnamed x10 -> x24, local copies, waits for them, and re-layouts: 0.03 us -> 5.59 us
  transfers between devices with their start and end apart: 1 -> 3, of which waited for: 1 -> 1; matrix products, arithmetic and copies ran while one was open for 5% -> 0% of each run, Pallas kernels for 0% -> 16%
where the time goes in v1:
time: 70.3 us; the launch traced here: 69.9 us
  blocking collectives  34.5 us (49%)
  Pallas kernels  19.9 us (28%)
  starting transfers between devices  7.58 us (11%)
  local copies, waits for them, and re-layouts  5.63 us (8%)
  waiting for transfers between devices  1.95 us (3%)
    all_to_all x2, blocking collectives, exchange(): lax.all_to_all(pieces, ('gx', 'gy'), 0, 0, axis_index_groups=groups, tile...  34.5 us
    pallas_call x2, Pallas kernels, inverse(): pl.pallas_call(functools.partial(inverse_kernel, side, steps), grid_spec=...  10.4 us
    pallas_call x2, Pallas kernels, forward(): pl.pallas_call(forward_kernel, grid_spec=pltpu.PrefetchScalarGridSpec(num...  7.28 us
    unnamed x24, local copies, waits for them, and re-layouts  5.59 us
    ppermute x1, starting transfers between devices, per_device(): other_sums = lax.ppermute(sums, 'gx', CORE_SWAP)  4.1 us
    pallas_call x1, Pallas kernels, inverse_tables(): pl.pallas_call(tables_kernel, in_specs=[smem, smem], out_shape=[jax.Shape...  2.2 us
    ppermute x1, starting transfers between devices, per_device(): piece = piece + lax.ppermute(piece, 'gx', Y_SWAP)  1.98 us
    ppermute x1, waiting for transfers between devices, per_device(): piece = piece + lax.ppermute(piece, 'gx', Y_SWAP)  1.94 us
  transfers between devices with their start and end apart: 3, of which 1 were waited for; matrix products, arithmetic and copies ran while one was open for 0% of the time, Pallas kernels for 16%

profile of v1, /device:TPU:1, one launch (start us, length us, event | category | flops | bytes accessed | tf_op | source)
XLA Modules:
  0.0 69.9 jit_solution(8196129493682677858)
XLA Ops:
  0.0 0.1 add_add_fusion.1.place_ref
  0.1 0.0 copy-start.1
  0.1 1.1 %copy-done.1 = bf16[16,64,384]{2,1,0:T(8,128)(2,1)S(1)} copy-done((bf16[16,64,384]{2,1,0:T(8,128)(2,1)S(1)}, bf16[16,64,384]{2,1,0:T(8,128)(2,1)}, u32[]{:S(2)}) %copy-start.1) | copy-done | bytes 786456
  1.2 0.0 copy-start.3
  1.2 1.0 %copy-done.3 = bf16[2048,128]{1,0:T(8,128)(2,1)S(1)} copy-done((bf16[2048,128]{1,0:T(8,128)(2,1)S(1)}, bf16[2048,128]{1,0:T(8,128)(2,1)}, u32[]{:S(2)}) %copy-start.3) | copy-done | bytes 524312
  2.3 0.0 copy-start.2
  2.3 0.0 copy-start.4
  2.3 3.5 %forward_modes.3 = f32[20,64,128]{2,1,0:T(8,128)S(1)} custom-call(s32[3]{0:T(128)S(1)} %add_add_fusion.1.place_ref, bf16[40,2,128,256]{3,2,1,0:T(8,128)(2,1)} %bitcast.13, bf16[2048,128]{1,0:T(8,128)(2,1)S(1)} %copy-done.3, bf16[16,64,384]{2,1,0:T(8,128)(2,1)S(1)} %copy-done.1), custom_call_target="tpu_custom_call" | custom-call | flops 167772160 | bytes 3276800 | tf_op jit(solution)/shard_map/forward_modes/pallas_call | solution.py:80
  5.8 1.5 %collective-permute-start = (f32[20,64,128]{2,1,0:T(8,128)S(1)}, f32[20,64,128]{2,1,0:T(8,128)S(1)}, u32[]{:S(2)}, u32[]{:S(2)}) collective-permute-start(f32[20,64,128]{2,1,0:T(8,128)S(1)} %forward_modes.3), channel_id=1, source_target_pairs={{0,16},{16,0},{32,48},{48,32},{64,80},{80,64},{96,112},{112,96},{1... | collective-permute-start | bytes 1966088 | tf_op jit(solution)/shard_map/ppermute | solution.py:279
  7.3 0.1 add_add_fusion.place_ref
  7.4 0.0 copy-done.2
  7.4 0.0 copy-done.4
  7.4 0.0 copy-start.8
  7.4 0.0 copy-start
  7.4 0.0 copy-start.10
  7.4 0.0 copy-start.11
  7.4 3.8 %forward_modes.2 = f32[20,64,128]{2,1,0:T(8,128)S(1)} custom-call(s32[3]{0:T(128)S(1)} %add_add_fusion.place_ref, bf16[40,2,128,256]{3,2,1,0:T(8,128)(2,1)} %bitcast.14, bf16[2048,128]{1,0:T(8,128)(2,1)S(1)} %copy-done.4, bf16[16,64,384]{2,1,0:T(8,128)(2,1)S(1)} %copy-done.2), custom_call_target="tpu_custom_call" | custom-call | flops 167772160 | bytes 3276800 | tf_op jit(solution)/shard_map/forward_modes/pallas_call | solution.py:80
  11.2 0.0 collective-permute-done
  11.2 0.1 add.6
  11.3 20.8 %all_to_all.10 = f32[32,40,128]{2,1,0:T(8,128)S(1)} all-to-all(f32[32,40,128]{2,1,0:T(8,128)S(1)} %bitcast.17), channel_id=1, replica_groups={{0,1,2,3,4,5,6,7,8,9,10,11,12,13,14,15,32,33,34,35,36,37,38,39,40,41,42..., dimensions={0} | all-to-all | bytes 1310720 | tf_op jit(solution)/shard_map/all_to_all | solution.py:284
  32.1 0.0 copy-done.8
  32.1 0.1 reduce_sum.9
  32.2 2.0 %collective-permute-start.1 = (f32[40,128]{1,0:T(8,128)S(1)}, f32[40,128]{1,0:T(8,128)S(1)}, u32[]{:S(2)}, u32[]{:S(2)}) collective-permute-start(f32[40,128]{1,0:T(8,128)S(1)} %reduce_sum.9), channel_id=1, source_target_pairs={{0,96},{16,112},{32,64},{48,80},{64,32},{80,48},{96,0},{112,16},{1... | collective-permute-start | bytes 61448 | tf_op jit(solution)/shard_map/ppermute | solution.py:287
  34.1 1.9 %collective-permute-done.1 = f32[40,128]{1,0:T(8,128)S(1)} collective-permute-done((f32[40,128]{1,0:T(8,128)S(1)}, f32[40,128]{1,0:T(8,128)S(1)}, u32[]{:S(2)}, u32[]{:S(2)}) %collective-permute-start.1) | collective-permute-done | bytes 20512 | tf_op jit(solution)/shard_map/ppermute | solution.py:287
  36.1 13.7 %all_to_all.11 = f32[32,40,128]{2,1,0:T(8,128)S(1)} all-to-all(f32[32,40,128]{2,1,0:T(8,128)S(1)} %broadcast_in_dim.2), channel_id=1, replica_groups={{0,1,2,3,4,5,6,7,8,9,10,11,12,13,14,15,32,33,34,35,36,37,38,39,40,41,42..., dimensions={0} | all-to-all | bytes 1310720 | tf_op jit(solution)/shard_map/all_to_all | solution.py:284
  49.8 4.1 %collective-permute-start.2 = (f32[20,64,128]{2,1,0:T(8,128)S(1)}, f32[20,64,128]{2,1,0:T(8,128)}, u32[]{:S(2)}, u32[]{:S(2)}) collective-permute-start(f32[20,64,128]{2,1,0:T(8,128)S(1)} %bitcast.11), channel_id=1, source_target_pairs={{0,16},{16,0},{32,48},{48,32},{64,80},{80,64},{96,112},{112,96},{1... | collective-permute-start | bytes 1966088 | tf_op jit(solution)/shard_map/ppermute | solution.py:291
  53.9 2.2 %inverse_tables.1 = (bf16[2,128,192]{2,1,0:T(8,128)(2,1)}, bf16[384,256]{1,0:T(8,128)(2,1)}, bf16[384,256]{1,0:T(8,128)(2,1)}) custom-call(s32[3]{0:T(128)} %copy-done.8, s32[2]{0:T(128)} %offset_ref.1), custom_call_target="tpu_custom_call" | custom-call | tf_op jit(solution)/shard_map/inverse_tables/pallas_call | solution.py:146
  56.1 0.0 copy-done
  56.1 0.0 copy-done.10
  56.1 0.0 copy-done.11
  56.1 0.0 copy-start.5
  56.1 0.9 %copy-done.5 = bf16[384,256]{1,0:T(8,128)(2,1)S(1)} copy-done((bf16[384,256]{1,0:T(8,128)(2,1)S(1)}, bf16[384,256]{1,0:T(8,128)(2,1)}, u32[]{:S(2)}) %copy-start.5) | copy-done | bytes 196632
  57.1 0.0 copy-start.6
  57.1 0.9 %copy-done.6 = bf16[384,256]{1,0:T(8,128)(2,1)S(1)} copy-done((bf16[384,256]{1,0:T(8,128)(2,1)S(1)}, bf16[384,256]{1,0:T(8,128)(2,1)}, u32[]{:S(2)}) %copy-start.6) | copy-done | bytes 196632
  58.0 0.0 copy-start.7
  58.0 0.9 %copy-done.7 = bf16[2,128,192]{2,1,0:T(8,128)(2,1)S(1)} copy-done((bf16[2,128,192]{2,1,0:T(8,128)(2,1)S(1)}, bf16[2,128,192]{2,1,0:T(8,128)(2,1)}, u32[]{:S(2)}) %copy-start.7) | copy-done | bytes 98328
  58.9 0.0 copy-start.9
  58.9 0.6 copy-done.9
  59.5 5.2 %inverse_own.1.rest_0_ = bf16[40,2,128,256]{3,2,1,0:T(8,128)(2,1)} custom-call(s32[3]{0:T(128)S(1)} %copy-done.9, s32[16]{0:T(128)S(1)} %copy-done.10, f32[5]{0:T(128)S(1)} %copy-done.11, bf16[40,2,128,256]{3,2,1,0:T(8,128)(2,1)} %bitcast.15, f32[20,64,128]{2,1,0:T(8,128)S(1)} %bitcast.12, f32[40,2,64,64]{3,2,1,0:T(8,128)S(1)} %bitcast.9, ...), custom_call_target="tpu_custom_call" | custom-call | flops 1006632960 | bytes 5898240 | tf_op jit(solution)/shard_map/inverse_own/pallas_call | solution.py:229
  64.7 0.0 collective-permute-done.2.modes_ref
  64.7 5.2 %inverse_other.1 = bf16[40,2,128,256]{3,2,1,0:T(8,128)(2,1)} custom-call(s32[3]{0:T(128)S(1)} %copy-done.9, s32[16]{0:T(128)S(1)} %copy-done.10, f32[5]{0:T(128)S(1)} %copy-done.11, bf16[40,2,128,256]{3,2,1,0:T(8,128)(2,1)} %bitcast.16, f32[20,64,128]{2,1,0:T(8,128)} %collective-permute-done.2.modes_ref, ...), custom_call_target="tpu_custom_call", output_to_operand_aliasing={{}: (9, {})} | custom-call | flops 1006632960 | bytes 5898240 | tf_op jit(solution)/shard_map/inverse_other/pallas_call | solution.py:229
  (2 shorter events, 0.1 us)
Async XLA Ops:
  0.1 1.1 %copy-start.1 = (bf16[16,64,384]{2,1,0:T(8,128)(2,1)S(1)}, bf16[16,64,384]{2,1,0:T(8,128)(2,1)}, u32[]{:S(2)}) copy-start(bf16[16,64,384]{2,1,0:T(8,128)(2,1)} %constant.18.clone.rows_ref) | copy-start | bytes 2359300
  1.2 1.0 %copy-start.3 = (bf16[2048,128]{1,0:T(8,128)(2,1)S(1)}, bf16[2048,128]{1,0:T(8,128)(2,1)}, u32[]{:S(2)}) copy-start(bf16[2048,128]{1,0:T(8,128)(2,1)} %constant.17.clone.cols_ref) | copy-start | bytes 1572868
  2.3 5.1 %copy-start.2 = (bf16[16,64,384]{2,1,0:T(8,128)(2,1)S(1)}, bf16[16,64,384]{2,1,0:T(8,128)(2,1)}, u32[]{:S(2)}) copy-start(bf16[16,64,384]{2,1,0:T(8,128)(2,1)} %constant.18.clone.rows_ref) | copy-start | bytes 2359300
  2.3 5.1 %copy-start.4 = (bf16[2048,128]{1,0:T(8,128)(2,1)S(1)}, bf16[2048,128]{1,0:T(8,128)(2,1)}, u32[]{:S(2)}) copy-start(bf16[2048,128]{1,0:T(8,128)(2,1)} %constant.17.clone.cols_ref) | copy-start | bytes 1572868
  5.8 5.4 %collective-permute-start = (f32[20,64,128]{2,1,0:T(8,128)S(1)}, f32[20,64,128]{2,1,0:T(8,128)S(1)}, u32[]{:S(2)}, u32[]{:S(2)}) collective-permute-start(f32[20,64,128]{2,1,0:T(8,128)S(1)} %forward_modes.3), channel_id=1, source_target_pairs={{0,16},{16,0},{32,48},{48,32},{64,80},{80,64},{96,112},{112,96},{1... | collective-permute-start | bytes 1966088 | tf_op jit(solution)/shard_map/ppermute | solution.py:279
  7.4 24.7 %copy-start.8 = (s32[3]{0:T(128)}, s32[3]{0:T(128)S(1)}, u32[]{:S(2)}) copy-start(s32[3]{0:T(128)S(1)} %add_add_fusion.place_ref) | copy-start | bytes 40
  7.4 48.7 %copy-start = (f32[5,16,64,64]{3,2,1,0:T(8,128)S(1)}, f32[5,16,64,64]{3,2,1,0:T(8,128)}, u32[]{:S(2)}) copy-start(f32[5,16,64,64]{3,2,1,0:T(8,128)} %param.8) | copy-start | bytes 3932164
  7.4 48.7 %copy-start.10 = (s32[16]{0:T(128)S(1)}, s32[16]{0:T(128)}, u32[]{:S(2)}) copy-start(s32[16]{0:T(128)} %mask_ref.3) | copy-start | bytes 196
  7.4 48.7 %copy-start.11 = (f32[5]{0:T(128)S(1)}, f32[5]{0:T(128)}, u32[]{:S(2)}) copy-start(f32[5]{0:T(128)} %gain_ref.3) | copy-start | bytes 64
  32.2 3.9 %collective-permute-start.1 = (f32[40,128]{1,0:T(8,128)S(1)}, f32[40,128]{1,0:T(8,128)S(1)}, u32[]{:S(2)}, u32[]{:S(2)}) collective-permute-start(f32[40,128]{1,0:T(8,128)S(1)} %reduce_sum.9), channel_id=1, source_target_pairs={{0,96},{16,112},{32,64},{48,80},{64,32},{80,48},{96,0},{112,16},{1... | collective-permute-start | bytes 61448 | tf_op jit(solution)/shard_map/ppermute | solution.py:287
  49.8 14.9 %collective-permute-start.2 = (f32[20,64,128]{2,1,0:T(8,128)S(1)}, f32[20,64,128]{2,1,0:T(8,128)}, u32[]{:S(2)}, u32[]{:S(2)}) collective-permute-start(f32[20,64,128]{2,1,0:T(8,128)S(1)} %bitcast.11), channel_id=1, source_target_pairs={{0,16},{16,0},{32,48},{48,32},{64,80},{80,64},{96,112},{112,96},{1... | collective-permute-start | bytes 1966088 | tf_op jit(solution)/shard_map/ppermute | solution.py:291
  56.1 0.9 %copy-start.5 = (bf16[384,256]{1,0:T(8,128)(2,1)S(1)}, bf16[384,256]{1,0:T(8,128)(2,1)}, u32[]{:S(2)}) copy-start(bf16[384,256]{1,0:T(8,128)(2,1)} %get-tuple-element.9.even_ref) | copy-start | bytes 589828
  57.1 0.9 %copy-start.6 = (bf16[384,256]{1,0:T(8,128)(2,1)S(1)}, bf16[384,256]{1,0:T(8,128)(2,1)}, u32[]{:S(2)}) copy-start(bf16[384,256]{1,0:T(8,128)(2,1)} %get-tuple-element.10.odd_ref) | copy-start | bytes 589828
  58.0 0.9 %copy-start.7 = (bf16[2,128,192]{2,1,0:T(8,128)(2,1)S(1)}, bf16[2,128,192]{2,1,0:T(8,128)(2,1)}, u32[]{:S(2)}) copy-start(bf16[2,128,192]{2,1,0:T(8,128)(2,1)} %get-tuple-element.8.rows_ref) | copy-start | bytes 294916
  58.9 0.6 copy-start.9

commit v2 on v0

v2 whole, which is shorter than its diff:
```python
import functools
import math

import jax
import jax.numpy as jnp
from jax import lax
from jax.experimental import pallas as pl
from jax.experimental.pallas import tpu as pltpu
from jax.sharding import PartitionSpec as P

MODES = 64
HALF = MODES // 2
CELLS = 2048
ROWS = 128
COLS = 256
SLABS = 80
LEVELS = 16
PAIRS = SLABS // 2
HALF_PAIRS = PAIRS // 2
EARLY = HALF_PAIRS // 2
INVERSE_OWN = (10, 10)
INVERSE_OTHER = (8, 8, 4)
HELD = INVERSE_OWN[-1]
TURN = 8
F32 = jnp.float32
BF16 = jnp.bfloat16
VMEM_LIMIT = 16 * 1024 * 1024
VMEM = pl.BlockSpec(memory_space=pltpu.VMEM)
SMEM = pl.BlockSpec(memory_space=pltpu.SMEM)
ANY = pl.BlockSpec(memory_space=pl.ANY)


def split_bf16(value):
    high = value.astype(BF16)
    low = (value - high.astype(F32)).astype(BF16)
    return high, low


def wave_number(mode):
    return jnp.where(mode < HALF, mode, mode - (HALF - 1))


def wave_value(mode, position):
    return wave_sine(wave_number(mode) * position + jnp.where(mode < HALF, CELLS // 4, 0))


def wave_sine(phase):
    phase = ((phase + CELLS // 2) & (CELLS - 1)) - CELLS // 2
    size = jnp.abs(phase)
    size = jnp.minimum(size, CELLS // 2 - size)
    angle = jnp.where(phase < 0, -size, size).astype(F32) * (2.0 * math.pi / CELLS)
    square = angle * angle
    total = jnp.full_like(square, 1.0 / math.factorial(13))
    for degree in (11, 9, 7, 5, 3, 1):
        sign = -1.0 if degree % 4 == 3 else 1.0
        total = total * square + sign / math.factorial(degree)
    return angle * total


def lane_mode(shape):
    return lax.broadcasted_iota(jnp.int32, shape, 1)


def row_index(shape):
    return lax.broadcasted_iota(jnp.int32, shape, 0)


def half_of(side):
    core = lax.axis_index("gx") & 1
    return core if side == 0 else 1 - core


def forward_tables(weight_ref, rows_ref):
    lane = lane_mode((COLS, 128))
    first_x = lax.axis_index("gx") * COLS
    table = wave_value(lane & (MODES - 1), row_index((COLS, 128)) + first_x)
    weight_ref[0:COLS, :] = jnp.where(lane < MODES, table, 0.0).astype(BF16)
    weight_ref[COLS:, :] = jnp.where(lane < MODES, 0.0, table).astype(BF16)
    first_y = lax.axis_index("gy") * ROWS
    shape = (MODES, ROWS)
    high, low = split_bf16(wave_value(row_index(shape), lane_mode(shape) + first_y))
    rows_ref[...] = jnp.concatenate([high, high, low], axis=1)


def forward_columns(tile_ref, source, span, weight_ref, high_ref, low_ref):
    pairs = span.stop - span.start
    left = tile_ref[source, 0].reshape(pairs * ROWS, COLS)
    right = tile_ref[source, 1].reshape(pairs * ROWS, COLS)
    along = jnp.dot(
        jnp.concatenate([left, right], axis=1), weight_ref[...], preferred_element_type=F32
    )
    high, low = split_bf16(along)
    high_ref[span] = high.reshape(pairs, ROWS, 128)
    low_ref[span] = low.reshape(pairs, ROWS, 128)


def forward_rows(span, rows_ref, high_ref, low_ref, out_ref):
    for pair in range(span.start, span.stop, 2):
        high = jnp.concatenate([high_ref[pair], high_ref[pair + 1]], axis=1)
        low = jnp.concatenate([low_ref[pair], low_ref[pair + 1]], axis=1)
        stacked = jnp.concatenate([high, low, high], axis=0)
        sums = jnp.dot(rows_ref[...], stacked, preferred_element_type=F32)
        out_ref[pair] = sums[:, 0:128]
        out_ref[pair + 1] = sums[:, 128:256]


def forward_other_kernel(
    field_ref, out_ref, own_ref, tile_ref, weight_ref, rows_ref, high_ref, low_ref, sems
):
    first_pair = half_of(1) * HALF_PAIRS
    copies = [
        pltpu.make_async_copy(
            field_ref.at[pl.ds(first_pair + index * EARLY, EARLY)],
            tile_ref.at[pl.ds(index * EARLY, EARLY)],
            sems.at[index],
        )
        for index in range(2)
    ]
    copies.append(
        pltpu.make_async_copy(
            field_ref.at[pl.ds(half_of(0) * HALF_PAIRS, EARLY)], own_ref, sems.at[2]
        )
    )
    for copy in copies:
        copy.start()
    forward_tables(weight_ref, rows_ref)
    for index in range(2):
        copies[index].wait()
        span = slice(index * EARLY, (index + 1) * EARLY)
        forward_columns(tile_ref, span, span, weight_ref, high_ref, low_ref)
    forward_rows(slice(0, HALF_PAIRS), rows_ref, high_ref, low_ref, out_ref)
    copies[2].wait()


def forward_own_kernel(
    field_ref, early_ref, out_ref, tile_ref, weight_ref, rows_ref, high_ref, low_ref, sem
):
    late = HALF_PAIRS - EARLY
    first_pair = half_of(0) * HALF_PAIRS + EARLY
    copy = pltpu.make_async_copy(field_ref.at[pl.ds(first_pair, late)], tile_ref, sem)
    copy.start()
    forward_tables(weight_ref, rows_ref)
    early_span, late_span = slice(0, EARLY), slice(EARLY, HALF_PAIRS)
    forward_columns(early_ref, early_span, early_span, weight_ref, high_ref, low_ref)
    forward_rows(early_span, rows_ref, high_ref, low_ref, out_ref)
    copy.wait()
    forward_columns(tile_ref, slice(0, late), late_span, weight_ref, high_ref, low_ref)
    forward_rows(late_span, rows_ref, high_ref, low_ref, out_ref)


def forward(side, field, early=None):
    out_shape = [pltpu.VMEM((HALF_PAIRS, MODES, 128), F32)]
    tile = HALF_PAIRS - EARLY
    if side == 1:
        out_shape.append(pltpu.VMEM((EARLY, 2, ROWS, COLS), BF16))
        tile = HALF_PAIRS
    return pl.pallas_call(
        forward_own_kernel if side == 0 else forward_other_kernel,
        in_specs=[ANY, VMEM] if side == 0 else [ANY],
        out_specs=[VMEM] * len(out_shape),
        out_shape=out_shape,
        scratch_shapes=[
            pltpu.VMEM((tile, 2, ROWS, COLS), BF16),
            pltpu.VMEM((2 * COLS, 128), BF16),
            pltpu.VMEM((MODES, 3 * ROWS), BF16),
            pltpu.VMEM((HALF_PAIRS, ROWS, 128), BF16),
            pltpu.VMEM((HALF_PAIRS, ROWS, 128), BF16),
            pltpu.SemaphoreType.DMA if side == 0 else pltpu.SemaphoreType.DMA((3,)),
        ],
        compiler_params=pltpu.CompilerParams(vmem_limit_bytes=VMEM_LIMIT),
        cost_estimate=pl.CostEstimate(
            flops=2 * HALF_PAIRS * 2 * ROWS * COLS * MODES,
            bytes_accessed=HALF_PAIRS * 2 * ROWS * COLS * 2 + HALF_PAIRS * MODES * 128 * 4,
            transcendentals=0,
        ),
        name="forward_own" if side == 0 else "forward_other",
    )(*([field] if side == 1 else [field, early]))


def turning_table(shift_x):
    shape = (128, 256)
    source, target = row_index(shape), lane_mode(shape)
    source_mode, mode = source & (MODES - 1), target & (MODES - 1)
    same = (source >= MODES) == ((target & 127) >= MODES)
    highest = target >= 128
    wave = jnp.where(highest, HALF, wave_number(mode))
    cosine = wave_sine(wave * shift_x + CELLS // 4)
    sine = wave_sine(wave * shift_x)
    to_cosine = (mode < HALF) & (source_mode == mode + (HALF - 1))
    to_sine = (mode >= HALF) & (source_mode == mode - (HALF - 1)) & (mode != MODES - 1)
    turned = jnp.where(to_cosine, sine, jnp.where(to_sine, -sine, 0.0))
    turned = jnp.where(source_mode == mode, cosine, turned)
    turned = jnp.where(same, turned, 0.0)
    last = jnp.where((source_mode == MODES - 1) & (mode < 3) & jnp.logical_not(same), sine, 0.0)
    return jnp.where(highest, last, turned)


def prepare_kernel(
    scalar_ref,
    parent_ref,
    after_ref,
    rows_ref,
    even_ref,
    odd_ref,
    gain_ref,
    along_ref,
    last_ref,
):
    del after_ref
    first_x = lax.axis_index("gx") * COLS
    first_y = lax.axis_index("gy") * ROWS
    shift_x = scalar_ref[0].astype(jnp.int32)
    shift_y = scalar_ref[1].astype(jnp.int32)
    shape = (ROWS, 128)
    lane = lane_mode(shape)
    mode = lane & (MODES - 1)
    position = row_index(shape) + first_y + jnp.where(lane < MODES, 0, shift_y)
    value = wave_value(mode, position)
    value = jnp.where((lane >= MODES) | (mode == 0), value, 2.0 * value)
    high, low = split_bf16(value)
    nest, parent = slice(0, MODES), slice(MODES, 128)
    rows_ref[...] = jnp.concatenate([high[:, nest], high[:, nest], low[:, nest]], axis=1)
    parent_rows = jnp.concatenate([high[:, parent], high[:, parent], low[:, parent]], axis=1)
    shape = (MODES, COLS)
    position = lane_mode(shape) + first_x
    high, low = split_bf16(wave_value(row_index(shape), position))
    highest = wave_sine(HALF * position + CELLS // 4)
    highest_high, highest_low = split_bf16(highest)
    row = row_index(shape)
    zero = jnp.zeros(shape, BF16)
    extra = jnp.where(row < 2, highest_high, jnp.where(row == 2, highest_low, zero))
    even_ref[...] = jnp.concatenate([high, high, low, extra], axis=0)
    odd_ref[...] = jnp.concatenate([high, high, extra, low], axis=0)
    high, low = split_bf16(turning_table(shift_x))
    turning = jnp.concatenate([high, high, low], axis=0)

    left = lane_mode((1, 128)) < MODES
    scale = jnp.where(lane_mode((1, 128)) & (MODES - 1) == 0, -1.0, -2.0) / (CELLS * CELLS)
    is_low = lane_mode((ROWS, 256)) & (MODES - 1) == 1
    for start in range(0, PAIRS, TURN):
        rows = []
        for pair in range(start, start + TURN):
            field, level = divmod(2 * pair, LEVELS)
            strength = scalar_ref[18 + field]
            gain = jnp.where(
                left, strength * scalar_ref[2 + level], strength * scalar_ref[3 + level]
            )
            gain_ref[pair : pair + 1, :] = gain * scale
            both = jnp.concatenate([parent_ref[pair, 0], parent_ref[pair, 1]], axis=1) * gain
            high, low = split_bf16(both)
            rows.append(jnp.concatenate([high, low, high], axis=1))
        turned = jnp.dot(jnp.concatenate(rows, axis=0), turning, preferred_element_type=F32)
        for pair in range(0, TURN, 2):
            first = turned[pair * MODES : (pair + 1) * MODES]
            second = turned[(pair + 1) * MODES : (pair + 2) * MODES]
            high, low = split_bf16(jnp.concatenate([first[:, 0:128], second[:, 0:128]], axis=1))
            stacked = jnp.concatenate([high, low, high], axis=0)
            along = jnp.dot(parent_rows, stacked, preferred_element_type=F32)
            high, low = split_bf16(jnp.concatenate([first[:, 128:], second[:, 128:]], axis=1))
            stacked = jnp.concatenate([high, low, high], axis=0)
            high, low = split_bf16(jnp.dot(parent_rows, stacked, preferred_element_type=F32))
            last = jnp.where(is_low, low, high)
            for slot in range(2):
                lanes = slice(slot * 128, (slot + 1) * 128)
                along_ref[start + pair + slot] = along[:, lanes]
                last_ref[start + pair + slot] = last[:, lanes]


def prepare(scalars, parent, after):
    return pl.pallas_call(
        prepare_kernel,
        in_specs=[SMEM, VMEM, ANY],
        out_specs=[VMEM] * 6,
        out_shape=[
            jax.ShapeDtypeStruct((ROWS, 3 * MODES), BF16),
            jax.ShapeDtypeStruct((4 * MODES, COLS), BF16),
            jax.ShapeDtypeStruct((4 * MODES, COLS), BF16),
            jax.ShapeDtypeStruct((PAIRS, 128), F32),
            jax.ShapeDtypeStruct((PAIRS, ROWS, 128), F32),
            jax.ShapeDtypeStruct((PAIRS, ROWS, 128), BF16),
        ],
        compiler_params=pltpu.CompilerParams(vmem_limit_bytes=VMEM_LIMIT),
        cost_estimate=pl.CostEstimate(
            flops=20 * PAIRS * ROWS * 128 * 3 * MODES,
            bytes_accessed=PAIRS * MODES * 128 * 8,
            transcendentals=0,
        ),
        name="parent_along_rows",
    )(scalars, parent, after)


def inverse_kernel(
    side, modes_ref, field_ref, rows_ref, even_ref, odd_ref, gain_ref, along_ref, last_ref, *rest
):
    first_pair = half_of(side) * HALF_PAIRS
    copies = []
    if side == 0:
        out_ref, held_ref, result_ref, left_ref, sems = rest
        chunks = INVERSE_OWN
    else:
        held_ref, _, out_ref, result_ref, left_ref, sems = rest
        chunks = INVERSE_OTHER
        first_held = half_of(0) * HALF_PAIRS + HALF_PAIRS - HELD
        copies.append(
            pltpu.make_async_copy(
                held_ref, out_ref.at[pl.ds(first_held, HELD)], sems.at[len(chunks)]
            )
        )
        copies[0].start()
    left = lane_mode((ROWS, 128)) < MODES
    for here in range(0, HALF_PAIRS, 2):
        nest = []
        for pair in (here, here + 1):
            nest.append(modes_ref[pair] * gain_ref[pl.ds(first_pair + pair, 1), :])
        high, low = split_bf16(jnp.concatenate(nest, axis=1))
        stacked = jnp.concatenate([high, low, high], axis=0)
        nest = jnp.dot(rows_ref[...], stacked, preferred_element_type=F32)
        for slot in range(2):
            pair = here + slot
            both = nest[:, slot * 128 : (slot + 1) * 128] + along_ref[first_pair + pair]
            high = both.astype(BF16)
            low = pltpu.roll(both - high.astype(F32), MODES, 1).astype(BF16)
            last = last_ref[first_pair + pair]
            left_ref[0, pair, :, 0:128] = jnp.where(left, high, low)
            left_ref[0, pair, :, 128:256] = jnp.where(left, high, last)
            left_ref[1, pair, :, 0:128] = jnp.where(left, low, high)
            left_ref[1, pair, :, 128:256] = jnp.where(left, last, high)
    start = 0
    for index, chunk in enumerate(chunks):
        span = slice(start, start + chunk)
        held = side == 0 and index == len(chunks) - 1
        for slot, table in enumerate((even_ref, odd_ref)):
            rows = left_ref[slot, span].reshape(chunk * ROWS, 256)
            correction = jnp.dot(rows, table[...], preferred_element_type=F32)
            correction = correction.reshape(chunk, ROWS, COLS)
            nudged = field_ref[pl.ds(first_pair + start, chunk), slot].astype(F32) + correction
            if held:
                held_ref[:, slot] = nudged.astype(BF16)
            else:
                result_ref[span, slot] = nudged.astype(BF16)
        if not held:
            copies.append(
                pltpu.make_async_copy(
                    result_ref.at[pl.ds(start, chunk)],
                    out_ref.at[pl.ds(first_pair + start, chunk)],
                    sems.at[index],
                )
            )
            copies[-1].start()
        start += chunk
    for copy in copies:
        copy.wait()


def inverse(side, modes, field, prepared, previous):
    operands = [modes, field, *prepared]
    in_specs = [VMEM] * len(operands)
    out_specs = [ANY]
    out_shape = [jax.ShapeDtypeStruct((PAIRS, 2, ROWS, COLS), BF16)]
    aliases = {}
    if side == 0:
        out_specs.append(VMEM)
        out_shape.append(pltpu.VMEM((HELD, 2, ROWS, COLS), BF16))
    else:
        out, held = previous
        operands += [held, out]
        in_specs += [VMEM, ANY]
        aliases = {len(operands) - 1: 0}
    return pl.pallas_call(
        functools.partial(inverse_kernel, side),
        in_specs=in_specs,
        out_specs=out_specs,
        out_shape=out_shape,
        scratch_shapes=[
            pltpu.VMEM((HALF_PAIRS, 2, ROWS, COLS), BF16),
            pltpu.VMEM((2, HALF_PAIRS, ROWS, 256), BF16),
            pltpu.SemaphoreType.DMA((4,)),
        ],
        input_output_aliases=aliases,
        compiler_params=pltpu.CompilerParams(vmem_limit_bytes=VMEM_LIMIT),
        cost_estimate=pl.CostEstimate(
            flops=2 * HALF_PAIRS * 2 * ROWS * COLS * 4 * MODES,
            bytes_accessed=HALF_PAIRS * 2 * ROWS * COLS * 4 + HALF_PAIRS * MODES * 128 * 4,
            transcendentals=0,
        ),
        name="inverse_own" if side == 0 else "inverse_other",
    )(*operands)


def device_index(y, core, row):
    return (2 * y + core) * 16 + row


def reduce_groups():
    return [
        [device_index(y, core, row) for y in pair for row in range(16)]
        for core in range(2)
        for pair in ((0, 1), (3, 2))
    ]


CORE_SWAP = [(i, i ^ 1) for i in range(8)]
Y_SWAP = [(2 * y + c, 2 * (3 - y) + c) for y in range(4) for c in range(2)]


def per_device(nest_fields, parent_modes, nest_offset, level_mask, strength):
    field = nest_fields.reshape(PAIRS, 2, ROWS, COLS)
    field = pltpu.with_memory_space_constraint(field, pltpu.HBM)
    parent = parent_modes.reshape(PAIRS, 2, MODES, MODES)
    scalars = jnp.concatenate([nest_offset.astype(F32), level_mask.astype(F32), strength])
    groups = reduce_groups()
    members = len(groups[0])

    for_partner, early = forward(1, field)
    from_partner = lax.ppermute(for_partner, "gx", CORE_SWAP)
    (own,) = forward(0, field, early)
    own = (own + from_partner).reshape(members, -1, 128)
    own, scalars = lax.optimization_barrier((own, scalars))

    def exchange(pieces):
        return lax.all_to_all(pieces, ("gx", "gy"), 0, 0, axis_index_groups=groups, tiled=True)

    piece = exchange(own).sum(0)
    from_pair = lax.ppermute(piece, "gx", Y_SWAP)
    prepared = prepare(scalars, parent, piece)
    from_pair, *prepared = lax.optimization_barrier((from_pair, *prepared))
    piece = piece + from_pair
    sums = exchange(jnp.broadcast_to(piece[None], (members,) + piece.shape))
    sums = sums.reshape(HALF_PAIRS, MODES, 128)
    other_sums = lax.ppermute(sums, "gx", CORE_SWAP)
    whole = nest_fields.reshape(PAIRS, 2, ROWS, COLS)
    previous = inverse(0, sums, whole, prepared, None)
    (out,) = inverse(1, other_sums, whole, prepared, previous)
    return out.reshape(nest_fields.shape)


def solution(mesh):
    in_specs = (P(None, None, "gy", "gx"), P(), P(), P(), P())
    out_specs = P(None, None, "gy", "gx")
    return jax.shard_map(
        per_device, mesh=mesh, in_specs=in_specs, out_specs=out_specs, check_vma=False
    )
```

time: 198 us -> 56.4 us (0.28)
  waiting for transfers between devices: 146 us -> 0.01 us
  matrix products: 35.5 us -> 0 us
  blocking collectives: 0 us -> 34.8 us
  Pallas kernels: 0 us -> 13.6 us
  between operations: 13.5 us -> 0.11 us
  starting transfers between devices: 0.01 us -> 7.34 us
    psum x1 -> x0, waiting for transfers between devices: 146 us -> none  [per_device(): mode_sums = lax.psum(partial_sums, ('gx', 'gy'))]
    dot_general x5 -> x0, matrix products: 35.5 us -> none  [the longest x1 13.6 us: per_device(): jnp.einsum('flkx,ky->flyx', stacked, row_tables, precision=highest)]
    all_to_all x0 -> x2, blocking collectives: none -> 34.8 us  [exchange(): lax.all_to_all(pieces, ('gx', 'gy'), 0, 0, axis_index_groups=groups, tile...]
    pallas_call x0 -> x5, Pallas kernels: none -> 13.6 us  [the longest x2 5.72 us: forward(): pl.pallas_call(forward_own_kernel if side == 0 else forward_other_kernel,...]
    ppermute x0 -> x3, starting transfers between devices: none -> 7.34 us  [the longest x1 3.85 us: per_device(): other_sums = lax.ppermute(sums, 'gx', CORE_SWAP)]
  transfers between devices with their start and end apart: 1 -> 3, of which waited for: 1 -> 0; matrix products, arithmetic and copies ran while one was open for 5% -> 0% of each run, Pallas kernels for 0% -> 13%
where the time goes in v2:
time: 56.4 us; the launch traced here: 56.2 us
  blocking collectives  34.8 us (62%)
  Pallas kernels  13.6 us (24%)
  starting transfers between devices  7.34 us (13%)
    all_to_all x2, blocking collectives, exchange(): lax.all_to_all(pieces, ('gx', 'gy'), 0, 0, axis_index_groups=groups, tile...  34.8 us
    pallas_call x2, Pallas kernels, forward(): pl.pallas_call(forward_own_kernel if side == 0 else forward_other_kernel,...  5.72 us
    pallas_call x2, Pallas kernels, inverse(): pl.pallas_call(functools.partial(inverse_kernel, side), in_specs=in_specs...  5.08 us
    ppermute x1, starting transfers between devices, per_device(): other_sums = lax.ppermute(sums, 'gx', CORE_SWAP)  3.85 us
    pallas_call x1, Pallas kernels, prepare(): pl.pallas_call(prepare_kernel, in_specs=[SMEM, VMEM, ANY], out_specs=[VME...  2.8 us
    ppermute x1, starting transfers between devices, per_device(): from_pair = lax.ppermute(piece, 'gx', Y_SWAP)  1.98 us
    ppermute x1, starting transfers between devices, per_device(): from_partner = lax.ppermute(for_partner, 'gx', CORE_SWAP)  1.5 us
  transfers between devices with their start and end apart: 3, of which 0 were waited for; matrix products, arithmetic and copies ran while one was open for 0% of the time, Pallas kernels for 13%

profile of v2, /device:TPU:1, one launch (start us, length us, event | category | flops | bytes accessed | tf_op | source)
XLA Modules:
  0.0 56.2 jit_solution(9543860377897186049)
XLA Ops:
  0.0 0.0 copy-start.2
  0.0 0.0 copy-start.3
  0.0 3.3 %forward_other.1 = (f32[20,64,128]{2,1,0:T(8,128)S(1)}, bf16[10,2,128,256]{3,2,1,0:T(8,128)(2,1)S(1)}) custom-call(bf16[40,2,128,256]{3,2,1,0:T(8,128)(2,1)} %bitcast.5), custom_call_target="tpu_custom_call" | custom-call | flops 167772160 | bytes 3276800 | tf_op jit(solution)/shard_map/forward_other/pallas_call | solution.py:157
  3.3 1.5 %collective-permute-start = (f32[20,64,128]{2,1,0:T(8,128)S(1)}, f32[20,64,128]{2,1,0:T(8,128)S(1)}, u32[]{:S(2)}, u32[]{:S(2)}) collective-permute-start(f32[20,64,128]{2,1,0:T(8,128)S(1)} %get-tuple-element.25), channel_id=1, source_target_pairs={{0,16},{16,0},{32,48},{48,32},{64,80},{80,64},{96,112},{112,96},{1... | collective-permute-start | bytes 1966088 | tf_op jit(solution)/shard_map/ppermute | solution.py:415
  4.8 0.0 copy-done.2
  4.8 0.0 copy-done.3
  4.8 0.0 copy-start.1
  4.9 2.4 %forward_own.1 = f32[20,64,128]{2,1,0:T(8,128)S(1)} custom-call(bf16[40,2,128,256]{3,2,1,0:T(8,128)(2,1)} %bitcast.6, bf16[10,2,128,256]{3,2,1,0:T(8,128)(2,1)S(1)} %get-tuple-element.24.early_ref), custom_call_target="tpu_custom_call" | custom-call | flops 167772160 | bytes 3276800 | tf_op jit(solution)/shard_map/forward_own/pallas_call | solution.py:157
  7.3 0.0 copy-done.1
  7.3 0.0 copy-start
  7.3 0.1 pad_maximum_fusion.scalar_ref
  7.4 0.0 collective-permute-done
  7.4 0.1 add.6
  7.5 20.8 %all_to_all.10 = f32[32,40,128]{2,1,0:T(8,128)S(1)} all-to-all(f32[32,40,128]{2,1,0:T(8,128)S(1)} %bitcast.14), channel_id=1, replica_groups={{0,1,2,3,4,5,6,7,8,9,10,11,12,13,14,15,32,33,34,35,36,37,38,39,40,41,42..., dimensions={0} | all-to-all | bytes 1310720 | tf_op jit(solution)/shard_map/all_to_all | solution.py:421
  28.3 0.1 reduce_sum.9.after_ref
  28.4 2.0 %collective-permute-start.1 = (f32[40,128]{1,0:T(8,128)S(1)}, f32[40,128]{1,0:T(8,128)S(1)}, u32[]{:S(2)}, u32[]{:S(2)}) collective-permute-start(f32[40,128]{1,0:T(8,128)S(1)} %reduce_sum.9.after_ref), channel_id=1, source_target_pairs={{0,96},{16,112},{32,64},{48,80},{64,32},{80,48},{96,0},{112,16},{1... | collective-permute-start | bytes 61448 | tf_op jit(solution)/shard_map/ppermute | solution.py:424
  30.3 0.0 slice-start
  30.3 0.0 copy-done
  30.3 0.0 slice-start.1
  30.3 2.8 %parent_along_rows.1 = (bf16[128,192]{1,0:T(8,128)(2,1)S(1)}, bf16[256,256]{1,0:T(8,128)(2,1)S(1)}, bf16[256,256]{1,0:T(8,128)(2,1)S(1)}, f32[40,128]{1,0:T(8,12...) custom-call(f32[23]{0:T(128)S(1)} %pad_maximum_fusion.scalar_ref, f32[40,2,64,64]{3,2,1,0:T(8,128)S(1)} %bitcast.13, ...), custom_call_target="tpu_custom_call" | custom-call | flops 2516582400 | bytes 2621440 | tf_op jit(solution)/shard_map/parent_along_rows/pallas_call | solution.py:270
  33.2 0.0 collective-permute-done.1
  33.2 14.0 %all_to_all.11 = f32[32,40,128]{2,1,0:T(8,128)S(1)} all-to-all(f32[32,40,128]{2,1,0:T(8,128)S(1)} %broadcast_in_dim.2), channel_id=1, replica_groups={{0,1,2,3,4,5,6,7,8,9,10,11,12,13,14,15,32,33,34,35,36,37,38,39,40,41,42..., dimensions={0} | all-to-all | bytes 1310720 | tf_op jit(solution)/shard_map/all_to_all | solution.py:421
  47.2 3.9 %collective-permute-start.2 = (f32[20,64,128]{2,1,0:T(8,128)S(1)}, f32[20,64,128]{2,1,0:T(8,128)S(1)}, u32[]{:S(2)}, u32[]{:S(2)}) collective-permute-start(f32[20,64,128]{2,1,0:T(8,128)S(1)} %bitcast.11), channel_id=1, source_target_pairs={{0,16},{16,0},{32,48},{48,32},{64,80},{80,64},{96,112},{112,96},{1... | collective-permute-start | bytes 1966088 | tf_op jit(solution)/shard_map/ppermute | solution.py:430
  51.1 0.0 slice-done
  51.1 0.0 slice-done.1
  51.1 2.3 %inverse_own.1 = (bf16[40,2,128,256]{3,2,1,0:T(8,128)(2,1)}, bf16[10,2,128,256]{3,2,1,0:T(8,128)(2,1)S(1)}) custom-call(f32[20,64,128]{2,1,0:T(8,128)S(1)} %bitcast.12, bf16[40,2,128,256]{3,2,1,0:T(8,128)(2,1)S(1)} %bitcast.9, bf16[128,192]{1,0:T(8,128)(2,1)S(1)} %get-tuple-element.35.rows_ref, bf16[256,256]{1,0:T(8,128)(2,1)S(1)} %get-tuple-element.36.even_ref, ...), custom_call_target="tpu_custom_call" | custom-call | flops 671088640 | bytes 5898240 | tf_op jit(solution)/shard_map/inverse_own/pallas_call | solution.py:369
  53.4 0.0 collective-permute-done.2.modes_ref
  53.4 2.8 %inverse_other.1 = bf16[40,2,128,256]{3,2,1,0:T(8,128)(2,1)} custom-call(f32[20,64,128]{2,1,0:T(8,128)S(1)} %collective-permute-done.2.modes_ref, bf16[40,2,128,256]{3,2,1,0:T(8,128)(2,1)S(1)} %bitcast.10, bf16[128,192]{1,0:T(8,128)(2,1)S(1)} %get-tuple-element.35.rows_ref, ...), custom_call_target="tpu_custom_call", output_to_operand_aliasing={{}: (9, {})} | custom-call | flops 671088640 | bytes 5898240 | tf_op jit(solution)/shard_map/inverse_other/pallas_call | solution.py:369
  (5 shorter events, 0.1 us)
Async XLA Ops:
  0.0 4.8 %copy-start.2 = (s32[2]{0:T(128)S(1)}, s32[2]{0:T(128)}, u32[]{:S(2)}) copy-start(s32[2]{0:T(128)} %param.7) | copy-start | bytes 28
  0.0 4.8 %copy-start.3 = (s32[16]{0:T(128)S(1)}, s32[16]{0:T(128)}, u32[]{:S(2)}) copy-start(s32[16]{0:T(128)} %param.8) | copy-start | bytes 196
  3.3 4.0 %collective-permute-start = (f32[20,64,128]{2,1,0:T(8,128)S(1)}, f32[20,64,128]{2,1,0:T(8,128)S(1)}, u32[]{:S(2)}, u32[]{:S(2)}) collective-permute-start(f32[20,64,128]{2,1,0:T(8,128)S(1)} %get-tuple-element.25), channel_id=1, source_target_pairs={{0,16},{16,0},{32,48},{48,32},{64,80},{80,64},{96,112},{112,96},{1... | collective-permute-start | bytes 1966088 | tf_op jit(solution)/shard_map/ppermute | solution.py:415
  4.8 2.4 %copy-start.1 = (f32[5]{0:T(128)S(1)}, f32[5]{0:T(128)}, u32[]{:S(2)}) copy-start(f32[5]{0:T(128)} %param.9) | copy-start | bytes 64
  7.3 23.1 %copy-start = (f32[5,16,64,64]{3,2,1,0:T(8,128)S(1)}, f32[5,16,64,64]{3,2,1,0:T(8,128)}, u32[]{:S(2)}) copy-start(f32[5,16,64,64]{3,2,1,0:T(8,128)} %param.6) | copy-start | bytes 3932164
  28.4 4.8 %collective-permute-start.1 = (f32[40,128]{1,0:T(8,128)S(1)}, f32[40,128]{1,0:T(8,128)S(1)}, u32[]{:S(2)}, u32[]{:S(2)}) collective-permute-start(f32[40,128]{1,0:T(8,128)S(1)} %reduce_sum.9.after_ref), channel_id=1, source_target_pairs={{0,96},{16,112},{32,64},{48,80},{64,32},{80,48},{96,0},{112,16},{1... | collective-permute-start | bytes 61448 | tf_op jit(solution)/shard_map/ppermute | solution.py:424
  30.3 20.7 %slice-start = ((s8[5242880]{0:T(1024)(128)(4,1)}), s8[4194304]{0:T(1024)(128)(4,1)S(1)}, s32[]{:S(2)}) async-start(s8[5242880]{0:T(1024)(128)(4,1)} %bitcast.7), calls=%async_computation.2 | async-start | bytes 8388608
  30.3 20.7 %slice-start.1 = ((s8[5242880]{0:T(1024)(128)(4,1)}), s8[1048576]{0:T(1024)(128)(4,1)S(1)}, s32[]{:S(2)}) async-start(s8[5242880]{0:T(1024)(128)(4,1)} %bitcast.7), calls=%async_computation.3 | async-start | bytes 2097152
  47.2 6.2 %collective-permute-start.2 = (f32[20,64,128]{2,1,0:T(8,128)S(1)}, f32[20,64,128]{2,1,0:T(8,128)S(1)}, u32[]{:S(2)}, u32[]{:S(2)}) collective-permute-start(f32[20,64,128]{2,1,0:T(8,128)S(1)} %bitcast.11), channel_id=1, source_target_pairs={{0,16},{16,0},{32,48},{48,32},{64,80},{80,64},{96,112},{112,96},{1... | collective-permute-start | bytes 1966088 | tf_op jit(solution)/shard_map/ppermute | solution.py:430

commit v3 on v2

--- a/solution.py
+++ b/solution.py
@@ -17,9 +17,8 @@
 LEVELS = 16
 PAIRS = SLABS // 2
 HALF_PAIRS = PAIRS // 2
-EARLY = HALF_PAIRS // 2
-INVERSE_OWN = (10, 10)
-INVERSE_OTHER = (8, 8, 4)
+INVERSE_OWN = (6, 8, 6)
+INVERSE_OTHER = (10, 6, 4)
 HELD = INVERSE_OWN[-1]
 TURN = 8
 F32 = jnp.float32
@@ -82,10 +81,10 @@
     rows_ref[...] = jnp.concatenate([high, high, low], axis=1)
 
 
-def forward_columns(tile_ref, source, span, weight_ref, high_ref, low_ref):
+def forward_columns(tile_ref, span, weight_ref, high_ref, low_ref):
     pairs = span.stop - span.start
-    left = tile_ref[source, 0].reshape(pairs * ROWS, COLS)
-    right = tile_ref[source, 1].reshape(pairs * ROWS, COLS)
+    left = tile_ref[span, 0].reshape(pairs * ROWS, COLS)
+    right = tile_ref[span, 1].reshape(pairs * ROWS, COLS)
     along = jnp.dot(
         jnp.concatenate([left, right], axis=1), weight_ref[...], preferred_element_type=F32
     )
@@ -94,8 +93,8 @@
     low_ref[span] = low.reshape(pairs, ROWS, 128)
 
 
-def forward_rows(span, rows_ref, high_ref, low_ref, out_ref):
-    for pair in range(span.start, span.stop, 2):
+def forward_rows(rows_ref, high_ref, low_ref, out_ref):
+    for pair in range(0, HALF_PAIRS, 2):
         high = jnp.concatenate([high_ref[pair], high_ref[pair + 1]], axis=1)
         low = jnp.concatenate([low_ref[pair], low_ref[pair + 1]], axis=1)
         stacked = jnp.concatenate([high, low, high], axis=0)
@@ -108,17 +107,18 @@
     field_ref, out_ref, own_ref, tile_ref, weight_ref, rows_ref, high_ref, low_ref, sems
 ):
     first_pair = half_of(1) * HALF_PAIRS
+    chunk = HALF_PAIRS // 2
     copies = [
         pltpu.make_async_copy(
-            field_ref.at[pl.ds(first_pair + index * EARLY, EARLY)],
-            tile_ref.at[pl.ds(index * EARLY, EARLY)],
+            field_ref.at[pl.ds(first_pair + index * chunk, chunk)],
+            tile_ref.at[pl.ds(index * chunk, chunk)],
             sems.at[index],
         )
         for index in range(2)
     ]
     copies.append(
         pltpu.make_async_copy(
-            field_ref.at[pl.ds(half_of(0) * HALF_PAIRS, EARLY)], own_ref, sems.at[2]
+            field_ref.at[pl.ds(half_of(0) * HALF_PAIRS, HALF_PAIRS)], own_ref, sems.at[2]
         )
     )
     for copy in copies:
@@ -126,47 +126,36 @@
     forward_tables(weight_ref, rows_ref)
     for index in range(2):
         copies[index].wait()
-        span = slice(index * EARLY, (index + 1) * EARLY)
-        forward_columns(tile_ref, span, span, weight_ref, high_ref, low_ref)
-    forward_rows(slice(0, HALF_PAIRS), rows_ref, high_ref, low_ref, out_ref)
+        span = slice(index * chunk, (index + 1) * chunk)
+        forward_columns(tile_ref, span, weight_ref, high_ref, low_ref)
+    forward_rows(rows_ref, high_ref, low_ref, out_ref)
     copies[2].wait()
 
 
-def forward_own_kernel(
-    field_ref, early_ref, out_ref, tile_ref, weight_ref, rows_ref, high_ref, low_ref, sem
-):
-    late = HALF_PAIRS - EARLY
-    first_pair = half_of(0) * HALF_PAIRS + EARLY
-    copy = pltpu.make_async_copy(field_ref.at[pl.ds(first_pair, late)], tile_ref, sem)
-    copy.start()
+def forward_own_kernel(tile_ref, out_ref, weight_ref, rows_ref, high_ref, low_ref):
     forward_tables(weight_ref, rows_ref)
-    early_span, late_span = slice(0, EARLY), slice(EARLY, HALF_PAIRS)
-    forward_columns(early_ref, early_span, early_span, weight_ref, high_ref, low_ref)
-    forward_rows(early_span, rows_ref, high_ref, low_ref, out_ref)
-    copy.wait()
-    forward_columns(tile_ref, slice(0, late), late_span, weight_ref, high_ref, low_ref)
-    forward_rows(late_span, rows_ref, high_ref, low_ref, out_ref)
-
-
-def forward(side, field, early=None):
+    forward_columns(tile_ref, slice(0, HALF_PAIRS), weight_ref, high_ref, low_ref)
+    forward_rows(rows_ref, high_ref, low_ref, out_ref)
+
+
+def forward(side, field):
+    tile = (HALF_PAIRS, 2, ROWS, COLS)
     out_shape = [pltpu.VMEM((HALF_PAIRS, MODES, 128), F32)]
-    tile = HALF_PAIRS - EARLY
+    scratch = [
+        pltpu.VMEM((2 * COLS, 128), BF16),
+        pltpu.VMEM((MODES, 3 * ROWS), BF16),
+        pltpu.VMEM((HALF_PAIRS, ROWS, 128), BF16),
+        pltpu.VMEM((HALF_PAIRS, ROWS, 128), BF16),
+    ]
     if side == 1:
-        out_shape.append(pltpu.VMEM((EARLY, 2, ROWS, COLS), BF16))
-        tile = HALF_PAIRS
+        out_shape.append(pltpu.VMEM(tile, BF16))
+        scratch = [pltpu.VMEM(tile, BF16), *scratch, pltpu.SemaphoreType.DMA((3,))]
     return pl.pallas_call(
         forward_own_kernel if side == 0 else forward_other_kernel,
-        in_specs=[ANY, VMEM] if side == 0 else [ANY],
+        in_specs=[VMEM if side == 0 else ANY],
         out_specs=[VMEM] * len(out_shape),
         out_shape=out_shape,
-        scratch_shapes=[
-            pltpu.VMEM((tile, 2, ROWS, COLS), BF16),
-            pltpu.VMEM((2 * COLS, 128), BF16),
-            pltpu.VMEM((MODES, 3 * ROWS), BF16),
-            pltpu.VMEM((HALF_PAIRS, ROWS, 128), BF16),
-            pltpu.VMEM((HALF_PAIRS, ROWS, 128), BF16),
-            pltpu.SemaphoreType.DMA if side == 0 else pltpu.SemaphoreType.DMA((3,)),
-        ],
+        scratch_shapes=scratch,
         compiler_params=pltpu.CompilerParams(vmem_limit_bytes=VMEM_LIMIT),
         cost_estimate=pl.CostEstimate(
             flops=2 * HALF_PAIRS * 2 * ROWS * COLS * MODES,
@@ -174,7 +163,7 @@
             transcendentals=0,
         ),
         name="forward_own" if side == 0 else "forward_other",
-    )(*([field] if side == 1 else [field, early]))
+    )(field)
 
 
 def turning_table(shift_x):
@@ -195,16 +184,8 @@
     return jnp.where(highest, last, turned)
 
 
-def prepare_kernel(
-    scalar_ref,
-    parent_ref,
-    after_ref,
-    rows_ref,
-    even_ref,
-    odd_ref,
-    gain_ref,
-    along_ref,
-    last_ref,
+def tables_kernel(
+    scalar_ref, after_ref, rows_ref, parent_rows_ref, even_ref, odd_ref, turning_ref, gain_ref
 ):
     del after_ref
     first_x = lax.axis_index("gx") * COLS
@@ -220,7 +201,9 @@
     high, low = split_bf16(value)
     nest, parent = slice(0, MODES), slice(MODES, 128)
     rows_ref[...] = jnp.concatenate([high[:, nest], high[:, nest], low[:, nest]], axis=1)
-    parent_rows = jnp.concatenate([high[:, parent], high[:, parent], low[:, parent]], axis=1)
+    parent_rows_ref[...] = jnp.concatenate(
+        [high[:, parent], high[:, parent], low[:, parent]], axis=1
+    )
     shape = (MODES, COLS)
     position = lane_mode(shape) + first_x
     high, low = split_bf16(wave_value(row_index(shape), position))
@@ -232,33 +215,42 @@
     even_ref[...] = jnp.concatenate([high, high, low, extra], axis=0)
     odd_ref[...] = jnp.concatenate([high, high, extra, low], axis=0)
     high, low = split_bf16(turning_table(shift_x))
-    turning = jnp.concatenate([high, high, low], axis=0)
-
+    turning_ref[...] = jnp.concatenate([high, high, low], axis=0)
     left = lane_mode((1, 128)) < MODES
-    scale = jnp.where(lane_mode((1, 128)) & (MODES - 1) == 0, -1.0, -2.0) / (CELLS * CELLS)
+    for pair in range(PAIRS):
+        field, level = divmod(2 * pair, LEVELS)
+        strength = scalar_ref[18 + field]
+        gain_ref[pair : pair + 1, :] = jnp.where(
+            left, strength * scalar_ref[2 + level], strength * scalar_ref[3 + level]
+        )
+
+
+def parent_kernel(
+    parent_ref, after_ref, parent_rows_ref, turning_ref, gain_ref, scaled_ref, along_ref, last_ref
+):
+    del after_ref
+    mode = lane_mode((PAIRS, 128)) & (MODES - 1)
+    scaled_ref[...] = gain_ref[...] * (jnp.where(mode == 0, -1.0, -2.0) / (CELLS * CELLS))
     is_low = lane_mode((ROWS, 256)) & (MODES - 1) == 1
     for start in range(0, PAIRS, TURN):
         rows = []
         for pair in range(start, start + TURN):
-            field, level = divmod(2 * pair, LEVELS)
-            strength = scalar_ref[18 + field]
-            gain = jnp.where(
-                left, strength * scalar_ref[2 + level], strength * scalar_ref[3 + level]
-            )
-            gain_ref[pair : pair + 1, :] = gain * scale
-            both = jnp.concatenate([parent_ref[pair, 0], parent_ref[pair, 1]], axis=1) * gain
-            high, low = split_bf16(both)
+            both = jnp.concatenate([parent_ref[pair, 0], parent_ref[pair, 1]], axis=1)
+            high, low = split_bf16(both * gain_ref[pair : pair + 1, :])
             rows.append(jnp.concatenate([high, low, high], axis=1))
-        turned = jnp.dot(jnp.concatenate(rows, axis=0), turning, preferred_element_type=F32)
+        turned = jnp.dot(
+            jnp.concatenate(rows, axis=0), turning_ref[...], preferred_element_type=F32
+        )
         for pair in range(0, TURN, 2):
             first = turned[pair * MODES : (pair + 1) * MODES]
             second = turned[(pair + 1) * MODES : (pair + 2) * MODES]
             high, low = split_bf16(jnp.concatenate([first[:, 0:128], second[:, 0:128]], axis=1))
             stacked = jnp.concatenate([high, low, high], axis=0)
-            along = jnp.dot(parent_rows, stacked, preferred_element_type=F32)
+            along = jnp.dot(parent_rows_ref[...], stacked, preferred_element_type=F32)
             high, low = split_bf16(jnp.concatenate([first[:, 128:], second[:, 128:]], axis=1))
             stacked = jnp.concatenate([high, low, high], axis=0)
-            high, low = split_bf16(jnp.dot(parent_rows, stacked, preferred_element_type=F32))
+            last = jnp.dot(parent_rows_ref[...], stacked, preferred_element_type=F32)
+            high, low = split_bf16(last)
             last = jnp.where(is_low, low, high)
             for slot in range(2):
                 lanes = slice(slot * 128, (slot + 1) * 128)
@@ -266,15 +258,30 @@
                 last_ref[start + pair + slot] = last[:, lanes]
 
 
-def prepare(scalars, parent, after):
+def make_tables(scalars, after):
     return pl.pallas_call(
-        prepare_kernel,
-        in_specs=[SMEM, VMEM, ANY],
+        tables_kernel,
+        in_specs=[SMEM, ANY],
         out_specs=[VMEM] * 6,
         out_shape=[
             jax.ShapeDtypeStruct((ROWS, 3 * MODES), BF16),
+            jax.ShapeDtypeStruct((ROWS, 3 * MODES), BF16),
             jax.ShapeDtypeStruct((4 * MODES, COLS), BF16),
             jax.ShapeDtypeStruct((4 * MODES, COLS), BF16),
+            jax.ShapeDtypeStruct((6 * MODES, 256), BF16),
+            jax.ShapeDtypeStruct((PAIRS, 128), F32),
+        ],
+        compiler_params=pltpu.CompilerParams(vmem_limit_bytes=VMEM_LIMIT),
+        name="tables",
+    )(scalars, after)
+
+
+def parent_along_rows(parent, after, parent_rows, turning, gain):
+    return pl.pallas_call(
+        parent_kernel,
+        in_specs=[VMEM, ANY, VMEM, VMEM, VMEM],
+        out_specs=[VMEM] * 3,
+        out_shape=[
             jax.ShapeDtypeStruct((PAIRS, 128), F32),
             jax.ShapeDtypeStruct((PAIRS, ROWS, 128), F32),
             jax.ShapeDtypeStruct((PAIRS, ROWS, 128), BF16),
@@ -286,7 +293,7 @@
             transcendentals=0,
         ),
         name="parent_along_rows",
-    )(scalars, parent, after)
+    )(parent, after, parent_rows, turning, gain)
 
 
 def inverse_kernel(
@@ -308,26 +315,26 @@
         )
         copies[0].start()
     left = lane_mode((ROWS, 128)) < MODES
-    for here in range(0, HALF_PAIRS, 2):
-        nest = []
-        for pair in (here, here + 1):
-            nest.append(modes_ref[pair] * gain_ref[pl.ds(first_pair + pair, 1), :])
-        high, low = split_bf16(jnp.concatenate(nest, axis=1))
-        stacked = jnp.concatenate([high, low, high], axis=0)
-        nest = jnp.dot(rows_ref[...], stacked, preferred_element_type=F32)
-        for slot in range(2):
-            pair = here + slot
-            both = nest[:, slot * 128 : (slot + 1) * 128] + along_ref[first_pair + pair]
-            high = both.astype(BF16)
-            low = pltpu.roll(both - high.astype(F32), MODES, 1).astype(BF16)
-            last = last_ref[first_pair + pair]
-            left_ref[0, pair, :, 0:128] = jnp.where(left, high, low)
-            left_ref[0, pair, :, 128:256] = jnp.where(left, high, last)
-            left_ref[1, pair, :, 0:128] = jnp.where(left, low, high)
-            left_ref[1, pair, :, 128:256] = jnp.where(left, last, high)
     start = 0
     for index, chunk in enumerate(chunks):
         span = slice(start, start + chunk)
+        for here in range(start, start + chunk, 2):
+            nest = []
+            for pair in (here, here + 1):
+                nest.append(modes_ref[pair] * gain_ref[pl.ds(first_pair + pair, 1), :])
+            high, low = split_bf16(jnp.concatenate(nest, axis=1))
+            stacked = jnp.concatenate([high, low, high], axis=0)
+            nest = jnp.dot(rows_ref[...], stacked, preferred_element_type=F32)
+            for slot in range(2):
+                pair = here + slot
+                both = nest[:, slot * 128 : (slot + 1) * 128] + along_ref[first_pair + pair]
+                high = both.astype(BF16)
+                low = pltpu.roll(both - high.astype(F32), MODES, 1).astype(BF16)
+                last = last_ref[first_pair + pair]
+                left_ref[0, pair, :, 0:128] = jnp.where(left, high, low)
+                left_ref[0, pair, :, 128:256] = jnp.where(left, high, last)
+                left_ref[1, pair, :, 0:128] = jnp.where(left, low, high)
+                left_ref[1, pair, :, 128:256] = jnp.where(left, last, high)
         held = side == 0 and index == len(chunks) - 1
         for slot, table in enumerate((even_ref, odd_ref)):
             rows = left_ref[slot, span].reshape(chunk * ROWS, 256)
@@ -387,20 +394,31 @@
     )(*operands)
 
 
-def device_index(y, core, row):
-    return (2 * y + core) * 16 + row
-
-
 def reduce_groups():
     return [
-        [device_index(y, core, row) for y in pair for row in range(16)]
+        [(2 * y + core) * 16 + 4 * z + x for z in pair for y in range(4) for x in range(4)]
         for core in range(2)
         for pair in ((0, 1), (3, 2))
     ]
 
 
 CORE_SWAP = [(i, i ^ 1) for i in range(8)]
-Y_SWAP = [(2 * y + c, 2 * (3 - y) + c) for y in range(4) for c in range(2)]
+Z_SWAP = [(4 * z + x, 4 * (3 - z) + x) for z in range(4) for x in range(4)]
+
+
+def sum_kernel(pieces_ref, out_ref):
+    out_ref[...] = jnp.sum(pieces_ref[...], axis=0)
+
+
+def sum_pieces(pieces):
+    return pl.pallas_call(
+        sum_kernel,
+        in_specs=[VMEM],
+        out_specs=VMEM,
+        out_shape=pltpu.VMEM(pieces.shape[1:], F32),
+        compiler_params=pltpu.CompilerParams(vmem_limit_bytes=VMEM_LIMIT),
+        name="sum_pieces",
+    )(pltpu.with_memory_space_constraint(pieces, pltpu.VMEM))
 
 
 def per_device(nest_fields, parent_modes, nest_offset, level_mask, strength):
@@ -411,19 +429,22 @@
     groups = reduce_groups()
     members = len(groups[0])
 
-    for_partner, early = forward(1, field)
+    for_partner, own_tile = forward(1, field)
     from_partner = lax.ppermute(for_partner, "gx", CORE_SWAP)
-    (own,) = forward(0, field, early)
+    (own,) = forward(0, own_tile)
+    tables = make_tables(scalars, own)
+    from_partner, tables = lax.optimization_barrier((from_partner, tables))
+    rows, parent_rows, even, odd, turning, gain = tables
     own = (own + from_partner).reshape(members, -1, 128)
-    own, scalars = lax.optimization_barrier((own, scalars))
 
     def exchange(pieces):
         return lax.all_to_all(pieces, ("gx", "gy"), 0, 0, axis_index_groups=groups, tiled=True)
 
-    piece = exchange(own).sum(0)
-    from_pair = lax.ppermute(piece, "gx", Y_SWAP)
-    prepared = prepare(scalars, parent, piece)
-    from_pair, *prepared = lax.optimization_barrier((from_pair, *prepared))
+    piece = sum_pieces(exchange(own))
+    from_pair = lax.ppermute(piece, "gy", Z_SWAP)
+    parents = parent_along_rows(parent, piece, parent_rows, turning, gain)
+    from_pair, parents = lax.optimization_barrier((from_pair, parents))
+    prepared = [rows, even, odd, *parents]
     piece = piece + from_pair
     sums = exchange(jnp.broadcast_to(piece[None], (members,) + piece.shape))
     sums = sums.reshape(HALF_PAIRS, MODES, 128)

time: 56.4 us -> 55.2 us (0.979)
  Pallas kernels: 13.6 us -> 12.8 us
    pallas_call x2, Pallas kernels: 5.72 us -> 4.86 us  [forward(): pl.pallas_call(forward_own_kernel if side == 0 else forward_other_kernel,...]
    pallas_call x1 -> x3, Pallas kernels: 2.8 us -> 3.02 us  [the longest x1 2.17 us: parent_along_rows(): pl.pallas_call(parent_kernel, in_specs=[VMEM, ANY, VMEM, VMEM, VMEM], out...]
where the time goes in v3:
time: 55.2 us; the launch traced here: 55 us
  blocking collectives  34.3 us (62%)
  Pallas kernels  12.8 us (23%)
  starting transfers between devices  7.46 us (14%)
    all_to_all x2, blocking collectives, exchange(): lax.all_to_all(pieces, ('gx', 'gy'), 0, 0, axis_index_groups=groups, tile...  34.3 us
    pallas_call x2, Pallas kernels, inverse(): pl.pallas_call(functools.partial(inverse_kernel, side), in_specs=in_specs...  4.94 us
    pallas_call x2, Pallas kernels, forward(): pl.pallas_call(forward_own_kernel if side == 0 else forward_other_kernel,...  4.86 us
    ppermute x1, starting transfers between devices, per_device(): other_sums = lax.ppermute(sums, 'gx', CORE_SWAP)  3.48 us
    ppermute x1, starting transfers between devices, per_device(): from_pair = lax.ppermute(piece, 'gy', Z_SWAP)  2.48 us
    pallas_call x1, Pallas kernels, parent_along_rows(): pl.pallas_call(parent_kernel, in_specs=[VMEM, ANY, VMEM, VMEM, VMEM], out...  2.17 us
    ppermute x1, starting transfers between devices, per_device(): from_partner = lax.ppermute(for_partner, 'gx', CORE_SWAP)  1.5 us
  transfers between devices with their start and end apart: 3, of which 0 were waited for; matrix products, arithmetic and copies ran while one was open for 0% of the time, Pallas kernels for 13%

profile of v3, /device:TPU:1, one launch (start us, length us, event | category | flops | bytes accessed | tf_op | source)
XLA Modules:
  0.0 55.0 jit_solution(17885403681131470867)
XLA Ops:
  0.0 0.0 copy-start.2
  0.0 0.0 copy-start.3
  0.0 3.3 %forward_other.1 = (f32[20,64,128]{2,1,0:T(8,128)S(1)}, bf16[20,2,128,256]{3,2,1,0:T(8,128)(2,1)S(1)}) custom-call(bf16[40,2,128,256]{3,2,1,0:T(8,128)(2,1)} %bitcast.5), custom_call_target="tpu_custom_call" | custom-call | flops 167772160 | bytes 3276800 | tf_op jit(solution)/shard_map/forward_other/pallas_call | solution.py:153
  3.3 0.0 copy-start.1
  3.3 1.5 %collective-permute-start = (f32[20,64,128]{2,1,0:T(8,128)S(1)}, f32[20,64,128]{2,1,0:T(8,128)S(1)}, u32[]{:S(2)}, u32[]{:S(2)}) collective-permute-start(f32[20,64,128]{2,1,0:T(8,128)S(1)} %get-tuple-element.30), channel_id=1, source_target_pairs={{0,16},{16,0},{32,48},{48,32},{64,80},{80,64},{96,112},{112,96},{1... | collective-permute-start | bytes 1966088 | tf_op jit(solution)/shard_map/ppermute | solution.py:433
  4.8 0.0 copy-done.2
  4.8 0.0 copy-done.3
  4.9 1.6 %forward_own.1.after_ref = f32[20,64,128]{2,1,0:T(8,128)S(1)} custom-call(bf16[20,2,128,256]{3,2,1,0:T(8,128)(2,1)S(1)} %get-tuple-element.29.tile_ref), custom_call_target="tpu_custom_call" | custom-call | flops 167772160 | bytes 3276800 | tf_op jit(solution)/shard_map/forward_own/pallas_call | solution.py:153
  6.4 0.0 copy-done.1
  6.4 0.0 copy-start
  6.4 0.1 pad_maximum_fusion.scalar_ref
  6.5 0.8 %tables.1 = (bf16[128,192]{1,0:T(8,128)(2,1)S(1)}, bf16[128,192]{1,0:T(8,128)(2,1)S(1)}, bf16[256,256]{1,0:T(8,128)(2,1)S(1)}, bf16[256,256]{1,0:T(8,128)(2,1)S(...) custom-call(f32[23]{0:T(128)S(1)} %pad_maximum_fusion.scalar_ref, f32[20,64,128]{2,1,0:T(8,128)S(1)} %forward_own.1.after_ref), custom_call_target="tpu_custom_call" | custom-call | tf_op jit(solution)/shard_map/tables/pallas_call | solution.py:262
  7.3 0.0 collective-permute-done
  7.3 0.1 add.6
  7.4 20.2 %all_to_all.10.pieces_ref = f32[32,40,128]{2,1,0:T(8,128)S(1)} all-to-all(f32[32,40,128]{2,1,0:T(8,128)S(1)} %bitcast.13), channel_id=1, replica_groups={{0,1,2,3,32,33,34,35,64,65,66,67,96,97,98,99,4,5,6,7,36,37,38,39,68,69,..., dimensions={0} | all-to-all | bytes 1310720 | tf_op jit(solution)/shard_map/all_to_all | solution.py:441
  27.6 0.1 sum_pieces.1.after_ref
  27.7 2.5 %collective-permute-start.1 = (f32[40,128]{1,0:T(8,128)S(1)}, f32[40,128]{1,0:T(8,128)S(1)}, u32[]{:S(2)}, u32[]{:S(2)}) collective-permute-start(f32[40,128]{1,0:T(8,128)S(1)} %sum_pieces.1.after_ref), channel_id=1, source_target_pairs={{0,12},{1,13},{2,14},{3,15},{4,8},{5,9},{6,10},{7,11},{8,4},{9,5},... | collective-permute-start | bytes 61448 | tf_op jit(solution)/shard_map/ppermute | solution.py:444
  30.2 0.0 slice-start
  30.2 0.0 copy-done
  30.2 0.0 slice-start.1
  30.2 2.2 %parent_along_rows.1 = (f32[40,128]{1,0:T(8,128)S(1)}, f32[40,128,128]{2,1,0:T(8,128)S(1)}, bf16[40,128,128]{2,1,0:T(8,128)(2,1)S(1)}) custom-call(f32[40,2,64,64]{3,2,1,0:T(8,128)S(1)} %bitcast.12, f32[40,128]{1,0:T(8,128)S(1)} %sum_pieces.1.after_ref, bf16[128,192]{1,0:T(8,128)(2,1)S(1)} %get-tuple-element.38.parent_rows_ref, ...), custom_call_target="tpu_custom_call" | custom-call | flops 2516582400 | bytes 2621440 | tf_op jit(solution)/shard_map/parent_along_rows/pallas_call | solution.py:280
  32.3 0.0 collective-permute-done.1
  32.4 14.1 %all_to_all.11 = f32[32,40,128]{2,1,0:T(8,128)S(1)} all-to-all(f32[32,40,128]{2,1,0:T(8,128)S(1)} %broadcast_in_dim.2), channel_id=1, replica_groups={{0,1,2,3,32,33,34,35,64,65,66,67,96,97,98,99,4,5,6,7,36,37,38,39,68,69,..., dimensions={0} | all-to-all | bytes 1310720 | tf_op jit(solution)/shard_map/all_to_all | solution.py:441
  46.5 3.5 %collective-permute-start.2 = (f32[20,64,128]{2,1,0:T(8,128)S(1)}, f32[20,64,128]{2,1,0:T(8,128)S(1)}, u32[]{:S(2)}, u32[]{:S(2)}) collective-permute-start(f32[20,64,128]{2,1,0:T(8,128)S(1)} %bitcast.10), channel_id=1, source_target_pairs={{0,16},{16,0},{32,48},{48,32},{64,80},{80,64},{96,112},{112,96},{1... | collective-permute-start | bytes 1966088 | tf_op jit(solution)/shard_map/ppermute | solution.py:451
  50.0 0.0 slice-done
  50.0 0.0 slice-done.1
  50.0 2.4 %inverse_own.1 = (bf16[40,2,128,256]{3,2,1,0:T(8,128)(2,1)}, bf16[6,2,128,256]{3,2,1,0:T(8,128)(2,1)S(1)}) custom-call(f32[20,64,128]{2,1,0:T(8,128)S(1)} %bitcast.11, bf16[40,2,128,256]{3,2,1,0:T(8,128)(2,1)S(1)} %bitcast.8, bf16[128,192]{1,0:T(8,128)(2,1)S(1)} %get-tuple-element.45.rows_ref, bf16[256,256]{1,0:T(8,128)(2,1)S(1)} %get-tuple-element.46.even_ref, ...), custom_call_target="tpu_custom_call" | custom-call | flops 671088640 | bytes 5898240 | tf_op jit(solution)/shard_map/inverse_own/pallas_call | solution.py:376
  52.4 0.0 collective-permute-done.2.modes_ref
  52.4 2.6 %inverse_other.1 = bf16[40,2,128,256]{3,2,1,0:T(8,128)(2,1)} custom-call(f32[20,64,128]{2,1,0:T(8,128)S(1)} %collective-permute-done.2.modes_ref, bf16[40,2,128,256]{3,2,1,0:T(8,128)(2,1)S(1)} %bitcast.9, bf16[128,192]{1,0:T(8,128)(2,1)S(1)} %get-tuple-element.45.rows_ref, ...), custom_call_target="tpu_custom_call", output_to_operand_aliasing={{}: (9, {})} | custom-call | flops 671088640 | bytes 5898240 | tf_op jit(solution)/shard_map/inverse_other/pallas_call | solution.py:376
  (5 shorter events, 0.1 us)
Async XLA Ops:
  0.0 4.8 %copy-start.2 = (s32[2]{0:T(128)S(1)}, s32[2]{0:T(128)}, u32[]{:S(2)}) copy-start(s32[2]{0:T(128)} %param.7) | copy-start | bytes 28
  0.0 4.8 %copy-start.3 = (s32[16]{0:T(128)S(1)}, s32[16]{0:T(128)}, u32[]{:S(2)}) copy-start(s32[16]{0:T(128)} %param.8) | copy-start | bytes 196
  3.3 3.1 %copy-start.1 = (f32[5]{0:T(128)S(1)}, f32[5]{0:T(128)}, u32[]{:S(2)}) copy-start(f32[5]{0:T(128)} %param.9) | copy-start | bytes 64
  3.3 4.0 %collective-permute-start = (f32[20,64,128]{2,1,0:T(8,128)S(1)}, f32[20,64,128]{2,1,0:T(8,128)S(1)}, u32[]{:S(2)}, u32[]{:S(2)}) collective-permute-start(f32[20,64,128]{2,1,0:T(8,128)S(1)} %get-tuple-element.30), channel_id=1, source_target_pairs={{0,16},{16,0},{32,48},{48,32},{64,80},{80,64},{96,112},{112,96},{1... | collective-permute-start | bytes 1966088 | tf_op jit(solution)/shard_map/ppermute | solution.py:433
  6.4 23.7 %copy-start = (f32[5,16,64,64]{3,2,1,0:T(8,128)S(1)}, f32[5,16,64,64]{3,2,1,0:T(8,128)}, u32[]{:S(2)}) copy-start(f32[5,16,64,64]{3,2,1,0:T(8,128)} %param.6) | copy-start | bytes 3932164
  27.7 4.7 %collective-permute-start.1 = (f32[40,128]{1,0:T(8,128)S(1)}, f32[40,128]{1,0:T(8,128)S(1)}, u32[]{:S(2)}, u32[]{:S(2)}) collective-permute-start(f32[40,128]{1,0:T(8,128)S(1)} %sum_pieces.1.after_ref), channel_id=1, source_target_pairs={{0,12},{1,13},{2,14},{3,15},{4,8},{5,9},{6,10},{7,11},{8,4},{9,5},... | collective-permute-start | bytes 61448 | tf_op jit(solution)/shard_map/ppermute | solution.py:444
  30.2 19.9 %slice-start = ((s8[5242880]{0:T(1024)(128)(4,1)}), s8[4194304]{0:T(1024)(128)(4,1)S(1)}, s32[]{:S(2)}) async-start(s8[5242880]{0:T(1024)(128)(4,1)} %bitcast.6), calls=%async_computation.2 | async-start | bytes 8388608
  30.2 19.9 %slice-start.1 = ((s8[5242880]{0:T(1024)(128)(4,1)}), s8[1048576]{0:T(1024)(128)(4,1)S(1)}, s32[]{:S(2)}) async-start(s8[5242880]{0:T(1024)(128)(4,1)} %bitcast.6), calls=%async_computation.3 | async-start | bytes 2097152
  46.5 5.9 %collective-permute-start.2 = (f32[20,64,128]{2,1,0:T(8,128)S(1)}, f32[20,64,128]{2,1,0:T(8,128)S(1)}, u32[]{:S(2)}, u32[]{:S(2)}) collective-permute-start(f32[20,64,128]{2,1,0:T(8,128)S(1)} %bitcast.10), channel_id=1, source_target_pairs={{0,16},{16,0},{32,48},{48,32},{64,80},{80,64},{96,112},{112,96},{1... | collective-permute-start | bytes 1966088 | tf_op jit(solution)/shard_map/ppermute | solution.py:451

commit v4 on v3

--- a/solution.py
+++ b/solution.py
@@ -132,13 +132,15 @@
     copies[2].wait()
 
 
-def forward_own_kernel(tile_ref, out_ref, weight_ref, rows_ref, high_ref, low_ref):
+def forward_own_kernel(tile_ref, scalar_ref, out_ref, *rest):
+    *tables, weight_ref, rows_ref, high_ref, low_ref = rest
     forward_tables(weight_ref, rows_ref)
     forward_columns(tile_ref, slice(0, HALF_PAIRS), weight_ref, high_ref, low_ref)
+    inverse_tables(scalar_ref, *tables)
     forward_rows(rows_ref, high_ref, low_ref, out_ref)
 
 
-def forward(side, field):
+def forward(side, field, scalars=None):
     tile = (HALF_PAIRS, 2, ROWS, COLS)
     out_shape = [pltpu.VMEM((HALF_PAIRS, MODES, 128), F32)]
     scratch = [
@@ -147,12 +149,21 @@
         pltpu.VMEM((HALF_PAIRS, ROWS, 128), BF16),
         pltpu.VMEM((HALF_PAIRS, ROWS, 128), BF16),
     ]
-    if side == 1:
+    if side == 0:
+        out_shape += [
+            jax.ShapeDtypeStruct((ROWS, 3 * MODES), BF16),
+            jax.ShapeDtypeStruct((ROWS, 3 * MODES), BF16),
+            jax.ShapeDtypeStruct((4 * MODES, COLS), BF16),
+            jax.ShapeDtypeStruct((4 * MODES, COLS), BF16),
+            jax.ShapeDtypeStruct((6 * MODES, 256), BF16),
+            jax.ShapeDtypeStruct((PAIRS, 128), F32),
+        ]
+    else:
         out_shape.append(pltpu.VMEM(tile, BF16))
         scratch = [pltpu.VMEM(tile, BF16), *scratch, pltpu.SemaphoreType.DMA((3,))]
     return pl.pallas_call(
         forward_own_kernel if side == 0 else forward_other_kernel,
-        in_specs=[VMEM if side == 0 else ANY],
+        in_specs=[VMEM, SMEM] if side == 0 else [ANY],
         out_specs=[VMEM] * len(out_shape),
         out_shape=out_shape,
         scratch_shapes=scratch,
@@ -163,7 +174,7 @@
             transcendentals=0,
         ),
         name="forward_own" if side == 0 else "forward_other",
-    )(field)
+    )(*([field, scalars] if side == 0 else [field]))
 
 
 def turning_table(shift_x):
@@ -184,10 +195,9 @@
     return jnp.where(highest, last, turned)
 
 
-def tables_kernel(
-    scalar_ref, after_ref, rows_ref, parent_rows_ref, even_ref, odd_ref, turning_ref, gain_ref
+def inverse_tables(
+    scalar_ref, rows_ref, parent_rows_ref, even_ref, odd_ref, turning_ref, gain_ref
 ):
-    del after_ref
     first_x = lax.axis_index("gx") * COLS
     first_y = lax.axis_index("gy") * ROWS
     shift_x = scalar_ref[0].astype(jnp.int32)
@@ -256,24 +266,6 @@
                 lanes = slice(slot * 128, (slot + 1) * 128)
                 along_ref[start + pair + slot] = along[:, lanes]
                 last_ref[start + pair + slot] = last[:, lanes]
-
-
-def make_tables(scalars, after):
-    return pl.pallas_call(
-        tables_kernel,
-        in_specs=[SMEM, ANY],
-        out_specs=[VMEM] * 6,
-        out_shape=[
-            jax.ShapeDtypeStruct((ROWS, 3 * MODES), BF16),
-            jax.ShapeDtypeStruct((ROWS, 3 * MODES), BF16),
-            jax.ShapeDtypeStruct((4 * MODES, COLS), BF16),
-            jax.ShapeDtypeStruct((4 * MODES, COLS), BF16),
-            jax.ShapeDtypeStruct((6 * MODES, 256), BF16),
-            jax.ShapeDtypeStruct((PAIRS, 128), F32),
-        ],
-        compiler_params=pltpu.CompilerParams(vmem_limit_bytes=VMEM_LIMIT),
-        name="tables",
-    )(scalars, after)
 
 
 def parent_along_rows(parent, after, parent_rows, turning, gain):
@@ -431,10 +423,7 @@
 
     for_partner, own_tile = forward(1, field)
     from_partner = lax.ppermute(for_partner, "gx", CORE_SWAP)
-    (own,) = forward(0, own_tile)
-    tables = make_tables(scalars, own)
-    from_partner, tables = lax.optimization_barrier((from_partner, tables))
-    rows, parent_rows, even, odd, turning, gain = tables
+    own, rows, parent_rows, even, odd, turning, gain = forward(0, own_tile, scalars)
     own = (own + from_partner).reshape(members, -1, 128)
 
     def exchange(pieces):

time: 55.2 us -> 55.2 us (level)
    pallas_call x1 -> x0, Pallas kernels: 0.8 us -> none  [make_tables(): pl.pallas_call(tables_kernel, in_specs=[SMEM, ANY], out_specs=[VMEM] * 6,...]
    pallas_call x2, Pallas kernels: 4.86 us -> 5.54 us  [forward(): pl.pallas_call(forward_own_kernel if side == 0 else forward_other_kernel,...]
  transfers between devices with their start and end apart: 3 -> 3, of which waited for: 0 -> 0; matrix products, arithmetic and copies ran while one was open for 0% -> 0% of each run, Pallas kernels for 13% -> 12%
where the time goes in v4:
time: 55.2 us; the launch traced here: 55 us
  blocking collectives  34.5 us (62%)
  Pallas kernels  12.7 us (23%)
  starting transfers between devices  7.42 us (13%)
    all_to_all x2, blocking collectives, exchange(): lax.all_to_all(pieces, ('gx', 'gy'), 0, 0, axis_index_groups=groups, tile...  34.5 us
    pallas_call x2, Pallas kernels, forward(): pl.pallas_call(forward_own_kernel if side == 0 else forward_other_kernel,...  5.54 us
    pallas_call x2, Pallas kernels, inverse(): pl.pallas_call(functools.partial(inverse_kernel, side), in_specs=in_specs...  4.94 us
    ppermute x1, starting transfers between devices, per_device(): other_sums = lax.ppermute(sums, 'gx', CORE_SWAP)  3.45 us
    ppermute x1, starting transfers between devices, per_device(): from_pair = lax.ppermute(piece, 'gy', Z_SWAP)  2.47 us
    pallas_call x1, Pallas kernels, parent_along_rows(): pl.pallas_call(parent_kernel, in_specs=[VMEM, ANY, VMEM, VMEM, VMEM], out...  2.21 us
    ppermute x1, starting transfers between devices, per_device(): from_partner = lax.ppermute(for_partner, 'gx', CORE_SWAP)  1.5 us
  transfers between devices with their start and end apart: 3, of which 0 were waited for; matrix products, arithmetic and copies ran while one was open for 0% of the time, Pallas kernels for 12%

profile of v4, /device:TPU:1, one launch (start us, length us, event | category | flops | bytes accessed | tf_op | source)
XLA Modules:
  0.0 55.0 jit_solution(10273791449790093280)
XLA Ops:
  0.0 0.0 copy-start.2
  0.0 0.0 copy-start.3
  0.0 0.0 copy-start.1
  0.0 3.3 %forward_other.1 = (f32[20,64,128]{2,1,0:T(8,128)S(1)}, bf16[20,2,128,256]{3,2,1,0:T(8,128)(2,1)S(1)}) custom-call(bf16[40,2,128,256]{3,2,1,0:T(8,128)(2,1)} %bitcast.5), custom_call_target="tpu_custom_call" | custom-call | flops 167772160 | bytes 3276800 | tf_op jit(solution)/shard_map/forward_other/pallas_call | solution.py:164
  3.3 1.5 %collective-permute-start = (f32[20,64,128]{2,1,0:T(8,128)S(1)}, f32[20,64,128]{2,1,0:T(8,128)S(1)}, u32[]{:S(2)}, u32[]{:S(2)}) collective-permute-start(f32[20,64,128]{2,1,0:T(8,128)S(1)} %get-tuple-element.25), channel_id=1, source_target_pairs={{0,16},{16,0},{32,48},{48,32},{64,80},{80,64},{96,112},{112,96},{1... | collective-permute-start | bytes 1966088 | tf_op jit(solution)/shard_map/ppermute | solution.py:425
  4.8 0.0 copy-done.2
  4.9 0.0 copy-done.3
  4.9 0.0 copy-done.1
  4.9 0.1 pad_maximum_fusion.scalar_ref
  4.9 2.2 %forward_own.1 = (f32[20,64,128]{2,1,0:T(8,128)S(1)}, bf16[128,192]{1,0:T(8,128)(2,1)S(1)}, bf16[128,192]{1,0:T(8,128)(2,1)S(1)}, bf16[256,256]{1,0:T(8,128)(2,1...) custom-call(bf16[20,2,128,256]{3,2,1,0:T(8,128)(2,1)S(1)} %get-tuple-element.23.tile_ref, ...), custom_call_target="tpu_custom_call" | custom-call | flops 167772160 | bytes 3276800 | tf_op jit(solution)/shard_map/forward_own/pallas_call | solution.py:164
  7.2 0.0 copy-start
  7.2 0.0 collective-permute-done
  7.2 0.1 add.6
  7.3 20.4 %all_to_all.10.pieces_ref = f32[32,40,128]{2,1,0:T(8,128)S(1)} all-to-all(f32[32,40,128]{2,1,0:T(8,128)S(1)} %bitcast.13), channel_id=1, replica_groups={{0,1,2,3,32,33,34,35,64,65,66,67,96,97,98,99,4,5,6,7,36,37,38,39,68,69,..., dimensions={0} | all-to-all | bytes 1310720 | tf_op jit(solution)/shard_map/all_to_all | solution.py:430
  27.6 0.1 sum_pieces.1.after_ref
  27.7 2.5 %collective-permute-start.1 = (f32[40,128]{1,0:T(8,128)S(1)}, f32[40,128]{1,0:T(8,128)S(1)}, u32[]{:S(2)}, u32[]{:S(2)}) collective-permute-start(f32[40,128]{1,0:T(8,128)S(1)} %sum_pieces.1.after_ref), channel_id=1, source_target_pairs={{0,12},{1,13},{2,14},{3,15},{4,8},{5,9},{6,10},{7,11},{8,4},{9,5},... | collective-permute-start | bytes 61448 | tf_op jit(solution)/shard_map/ppermute | solution.py:433
  30.1 0.0 slice-start
  30.1 0.0 copy-done
  30.2 0.0 slice-start.1
  30.2 2.2 %parent_along_rows.1 = (f32[40,128]{1,0:T(8,128)S(1)}, f32[40,128,128]{2,1,0:T(8,128)S(1)}, bf16[40,128,128]{2,1,0:T(8,128)(2,1)S(1)}) custom-call(f32[40,2,64,64]{3,2,1,0:T(8,128)S(1)} %bitcast.12, f32[40,128]{1,0:T(8,128)S(1)} %sum_pieces.1.after_ref, bf16[128,192]{1,0:T(8,128)(2,1)S(1)} %get-tuple-element.26.parent_rows_ref, ...), custom_call_target="tpu_custom_call" | custom-call | flops 2516582400 | bytes 2621440 | tf_op jit(solution)/shard_map/parent_along_rows/pallas_call | solution.py:272
  32.4 0.0 collective-permute-done.1
  32.4 14.1 %all_to_all.11 = f32[32,40,128]{2,1,0:T(8,128)S(1)} all-to-all(f32[32,40,128]{2,1,0:T(8,128)S(1)} %broadcast_in_dim.2), channel_id=1, replica_groups={{0,1,2,3,32,33,34,35,64,65,66,67,96,97,98,99,4,5,6,7,36,37,38,39,68,69,..., dimensions={0} | all-to-all | bytes 1310720 | tf_op jit(solution)/shard_map/all_to_all | solution.py:430
  46.6 3.5 %collective-permute-start.2 = (f32[20,64,128]{2,1,0:T(8,128)S(1)}, f32[20,64,128]{2,1,0:T(8,128)S(1)}, u32[]{:S(2)}, u32[]{:S(2)}) collective-permute-start(f32[20,64,128]{2,1,0:T(8,128)S(1)} %bitcast.10), channel_id=1, source_target_pairs={{0,16},{16,0},{32,48},{48,32},{64,80},{80,64},{96,112},{112,96},{1... | collective-permute-start | bytes 1966088 | tf_op jit(solution)/shard_map/ppermute | solution.py:440
  50.0 0.0 slice-done
  50.0 0.0 slice-done.1
  50.0 2.4 %inverse_own.1 = (bf16[40,2,128,256]{3,2,1,0:T(8,128)(2,1)}, bf16[6,2,128,256]{3,2,1,0:T(8,128)(2,1)S(1)}) custom-call(f32[20,64,128]{2,1,0:T(8,128)S(1)} %bitcast.11, bf16[40,2,128,256]{3,2,1,0:T(8,128)(2,1)S(1)} %bitcast.8, bf16[128,192]{1,0:T(8,128)(2,1)S(1)} %get-tuple-element.33.rows_ref, bf16[256,256]{1,0:T(8,128)(2,1)S(1)} %get-tuple-element.34.even_ref, ...), custom_call_target="tpu_custom_call" | custom-call | flops 671088640 | bytes 5898240 | tf_op jit(solution)/shard_map/inverse_own/pallas_call | solution.py:368
  52.4 0.0 collective-permute-done.2.modes_ref
  52.4 2.6 %inverse_other.1 = bf16[40,2,128,256]{3,2,1,0:T(8,128)(2,1)} custom-call(f32[20,64,128]{2,1,0:T(8,128)S(1)} %collective-permute-done.2.modes_ref, bf16[40,2,128,256]{3,2,1,0:T(8,128)(2,1)S(1)} %bitcast.9, bf16[128,192]{1,0:T(8,128)(2,1)S(1)} %get-tuple-element.33.rows_ref, ...), custom_call_target="tpu_custom_call", output_to_operand_aliasing={{}: (9, {})} | custom-call | flops 671088640 | bytes 5898240 | tf_op jit(solution)/shard_map/inverse_other/pallas_call | solution.py:368
  (5 shorter events, 0.1 us)
Async XLA Ops:
  0.0 4.8 %copy-start.2 = (s32[2]{0:T(128)S(1)}, s32[2]{0:T(128)}, u32[]{:S(2)}) copy-start(s32[2]{0:T(128)} %param.7) | copy-start | bytes 28
  0.0 4.8 %copy-start.3 = (s32[16]{0:T(128)S(1)}, s32[16]{0:T(128)}, u32[]{:S(2)}) copy-start(s32[16]{0:T(128)} %param.8) | copy-start | bytes 196
  0.0 4.9 %copy-start.1 = (f32[5]{0:T(128)S(1)}, f32[5]{0:T(128)}, u32[]{:S(2)}) copy-start(f32[5]{0:T(128)} %param.9) | copy-start | bytes 64
  3.3 3.8 %collective-permute-start = (f32[20,64,128]{2,1,0:T(8,128)S(1)}, f32[20,64,128]{2,1,0:T(8,128)S(1)}, u32[]{:S(2)}, u32[]{:S(2)}) collective-permute-start(f32[20,64,128]{2,1,0:T(8,128)S(1)} %get-tuple-element.25), channel_id=1, source_target_pairs={{0,16},{16,0},{32,48},{48,32},{64,80},{80,64},{96,112},{112,96},{1... | collective-permute-start | bytes 1966088 | tf_op jit(solution)/shard_map/ppermute | solution.py:425
  7.2 23.0 %copy-start = (f32[5,16,64,64]{3,2,1,0:T(8,128)S(1)}, f32[5,16,64,64]{3,2,1,0:T(8,128)}, u32[]{:S(2)}) copy-start(f32[5,16,64,64]{3,2,1,0:T(8,128)} %param.6) | copy-start | bytes 3932164
  27.7 4.7 %collective-permute-start.1 = (f32[40,128]{1,0:T(8,128)S(1)}, f32[40,128]{1,0:T(8,128)S(1)}, u32[]{:S(2)}, u32[]{:S(2)}) collective-permute-start(f32[40,128]{1,0:T(8,128)S(1)} %sum_pieces.1.after_ref), channel_id=1, source_target_pairs={{0,12},{1,13},{2,14},{3,15},{4,8},{5,9},{6,10},{7,11},{8,4},{9,5},... | collective-permute-start | bytes 61448 | tf_op jit(solution)/shard_map/ppermute | solution.py:433
  30.1 19.9 %slice-start = ((s8[5242880]{0:T(1024)(128)(4,1)}), s8[4194304]{0:T(1024)(128)(4,1)S(1)}, s32[]{:S(2)}) async-start(s8[5242880]{0:T(1024)(128)(4,1)} %bitcast.6), calls=%async_computation.2 | async-start | bytes 8388608
  30.2 19.9 %slice-start.1 = ((s8[5242880]{0:T(1024)(128)(4,1)}), s8[1048576]{0:T(1024)(128)(4,1)S(1)}, s32[]{:S(2)}) async-start(s8[5242880]{0:T(1024)(128)(4,1)} %bitcast.6), calls=%async_computation.3 | async-start | bytes 2097152
  46.6 5.9 %collective-permute-start.2 = (f32[20,64,128]{2,1,0:T(8,128)S(1)}, f32[20,64,128]{2,1,0:T(8,128)S(1)}, u32[]{:S(2)}, u32[]{:S(2)}) collective-permute-start(f32[20,64,128]{2,1,0:T(8,128)S(1)} %bitcast.10), channel_id=1, source_target_pairs={{0,16},{16,0},{32,48},{48,32},{64,80},{80,64},{96,112},{112,96},{1... | collective-permute-start | bytes 1966088 | tf_op jit(solution)/shard_map/ppermute | solution.py:440

commit v5 on v4

--- a/solution.py
+++ b/solution.py
@@ -388,14 +388,14 @@
 
 def reduce_groups():
     return [
-        [(2 * y + core) * 16 + 4 * z + x for z in pair for y in range(4) for x in range(4)]
+        [(2 * y + core) * 16 + 4 * z + x for x in pair for y in range(4) for z in range(4)]
         for core in range(2)
         for pair in ((0, 1), (3, 2))
     ]
 
 
 CORE_SWAP = [(i, i ^ 1) for i in range(8)]
-Z_SWAP = [(4 * z + x, 4 * (3 - z) + x) for z in range(4) for x in range(4)]
+X_SWAP = [(4 * z + x, 4 * z + 3 - x) for z in range(4) for x in range(4)]
 
 
 def sum_kernel(pieces_ref, out_ref):
@@ -430,7 +430,7 @@
         return lax.all_to_all(pieces, ("gx", "gy"), 0, 0, axis_index_groups=groups, tiled=True)
 
     piece = sum_pieces(exchange(own))
-    from_pair = lax.ppermute(piece, "gy", Z_SWAP)
+    from_pair = lax.ppermute(piece, "gy", X_SWAP)
     parents = parent_along_rows(parent, piece, parent_rows, turning, gain)
     from_pair, parents = lax.optimization_barrier((from_pair, parents))
     prepared = [rows, even, odd, *parents]

time: 55.2 us -> 55.1 us (level)
    ppermute x1, starting transfers between devices: 3.45 us -> 4.07 us  [per_device(): other_sums = lax.ppermute(sums, 'gx', CORE_SWAP)]
    ppermute x1, starting transfers between devices: 2.47 us -> 1.88 us  [per_device(): from_pair = lax.ppermute(piece, 'gy', X_SWAP)]
where the time goes in v5:
time: 55.1 us; the launch traced here: 54.9 us
  blocking collectives  34.4 us (62%)
  Pallas kernels  12.7 us (23%)
  starting transfers between devices  7.45 us (14%)
    all_to_all x2, blocking collectives, exchange(): lax.all_to_all(pieces, ('gx', 'gy'), 0, 0, axis_index_groups=groups, tile...  34.4 us
    pallas_call x2, Pallas kernels, forward(): pl.pallas_call(forward_own_kernel if side == 0 else forward_other_kernel,...  5.54 us
    pallas_call x2, Pallas kernels, inverse(): pl.pallas_call(functools.partial(inverse_kernel, side), in_specs=in_specs...  4.94 us
    ppermute x1, starting transfers between devices, per_device(): other_sums = lax.ppermute(sums, 'gx', CORE_SWAP)  4.07 us
    pallas_call x1, Pallas kernels, parent_along_rows(): pl.pallas_call(parent_kernel, in_specs=[VMEM, ANY, VMEM, VMEM, VMEM], out...  2.21 us
    ppermute x1, starting transfers between devices, per_device(): from_pair = lax.ppermute(piece, 'gy', X_SWAP)  1.88 us
    ppermute x1, starting transfers between devices, per_device(): from_partner = lax.ppermute(for_partner, 'gx', CORE_SWAP)  1.5 us
  transfers between devices with their start and end apart: 3, of which 0 were waited for; matrix products, arithmetic and copies ran while one was open for 0% of the time, Pallas kernels for 12%

profile of v5, /device:TPU:1, one launch (start us, length us, event | category | flops | bytes accessed | tf_op | source)
XLA Modules:
  0.0 54.9 jit_solution(12971241223280803668)
XLA Ops:
  0.0 0.0 copy-start.2
  0.0 0.0 copy-start.3
  0.0 0.0 copy-start.1
  0.0 3.3 %forward_other.1 = (f32[20,64,128]{2,1,0:T(8,128)S(1)}, bf16[20,2,128,256]{3,2,1,0:T(8,128)(2,1)S(1)}) custom-call(bf16[40,2,128,256]{3,2,1,0:T(8,128)(2,1)} %bitcast.5), custom_call_target="tpu_custom_call" | custom-call | flops 167772160 | bytes 3276800 | tf_op jit(solution)/shard_map/forward_other/pallas_call | solution.py:164
  3.3 1.5 %collective-permute-start = (f32[20,64,128]{2,1,0:T(8,128)S(1)}, f32[20,64,128]{2,1,0:T(8,128)S(1)}, u32[]{:S(2)}, u32[]{:S(2)}) collective-permute-start(f32[20,64,128]{2,1,0:T(8,128)S(1)} %get-tuple-element.25), channel_id=1, source_target_pairs={{0,16},{16,0},{32,48},{48,32},{64,80},{80,64},{96,112},{112,96},{1... | collective-permute-start | bytes 1966088 | tf_op jit(solution)/shard_map/ppermute | solution.py:425
  4.8 0.0 copy-done.2
  4.9 0.0 copy-done.3
  4.9 0.0 copy-done.1
  4.9 0.1 pad_maximum_fusion.scalar_ref
  4.9 2.2 %forward_own.1 = (f32[20,64,128]{2,1,0:T(8,128)S(1)}, bf16[128,192]{1,0:T(8,128)(2,1)S(1)}, bf16[128,192]{1,0:T(8,128)(2,1)S(1)}, bf16[256,256]{1,0:T(8,128)(2,1...) custom-call(bf16[20,2,128,256]{3,2,1,0:T(8,128)(2,1)S(1)} %get-tuple-element.23.tile_ref, ...), custom_call_target="tpu_custom_call" | custom-call | flops 167772160 | bytes 3276800 | tf_op jit(solution)/shard_map/forward_own/pallas_call | solution.py:164
  7.2 0.0 copy-start
  7.2 0.0 collective-permute-done
  7.2 0.1 add.6
  7.3 20.7 %all_to_all.10.pieces_ref = f32[32,40,128]{2,1,0:T(8,128)S(1)} all-to-all(f32[32,40,128]{2,1,0:T(8,128)S(1)} %bitcast.13), channel_id=1, replica_groups={{0,4,8,12,32,36,40,44,64,68,72,76,96,100,104,108,1,5,9,13,33,37,41,45,6..., dimensions={0} | all-to-all | bytes 1310720 | tf_op jit(solution)/shard_map/all_to_all | solution.py:430
  27.9 0.1 sum_pieces.1.after_ref
  28.0 1.9 %collective-permute-start.1 = (f32[40,128]{1,0:T(8,128)S(1)}, f32[40,128]{1,0:T(8,128)S(1)}, u32[]{:S(2)}, u32[]{:S(2)}) collective-permute-start(f32[40,128]{1,0:T(8,128)S(1)} %sum_pieces.1.after_ref), channel_id=1, source_target_pairs={{0,3},{1,2},{2,1},{3,0},{4,7},{5,6},{6,5},{7,4},{8,11},{9,10},{10,... | collective-permute-start | bytes 61448 | tf_op jit(solution)/shard_map/ppermute | solution.py:433
  29.9 0.0 slice-start
  29.9 0.0 copy-done
  29.9 0.0 slice-start.1
  29.9 2.2 %parent_along_rows.1 = (f32[40,128]{1,0:T(8,128)S(1)}, f32[40,128,128]{2,1,0:T(8,128)S(1)}, bf16[40,128,128]{2,1,0:T(8,128)(2,1)S(1)}) custom-call(f32[40,2,64,64]{3,2,1,0:T(8,128)S(1)} %bitcast.12, f32[40,128]{1,0:T(8,128)S(1)} %sum_pieces.1.after_ref, bf16[128,192]{1,0:T(8,128)(2,1)S(1)} %get-tuple-element.26.parent_rows_ref, ...), custom_call_target="tpu_custom_call" | custom-call | flops 2516582400 | bytes 2621440 | tf_op jit(solution)/shard_map/parent_along_rows/pallas_call | solution.py:272
  32.1 0.0 collective-permute-done.1
  32.2 13.7 %all_to_all.11 = f32[32,40,128]{2,1,0:T(8,128)S(1)} all-to-all(f32[32,40,128]{2,1,0:T(8,128)S(1)} %broadcast_in_dim.2), channel_id=1, replica_groups={{0,4,8,12,32,36,40,44,64,68,72,76,96,100,104,108,1,5,9,13,33,37,41,45,6..., dimensions={0} | all-to-all | bytes 1310720 | tf_op jit(solution)/shard_map/all_to_all | solution.py:430
  45.9 4.1 %collective-permute-start.2 = (f32[20,64,128]{2,1,0:T(8,128)S(1)}, f32[20,64,128]{2,1,0:T(8,128)S(1)}, u32[]{:S(2)}, u32[]{:S(2)}) collective-permute-start(f32[20,64,128]{2,1,0:T(8,128)S(1)} %bitcast.10), channel_id=1, source_target_pairs={{0,16},{16,0},{32,48},{48,32},{64,80},{80,64},{96,112},{112,96},{1... | collective-permute-start | bytes 1966088 | tf_op jit(solution)/shard_map/ppermute | solution.py:440
  50.0 0.0 slice-done
  50.0 0.0 slice-done.1
  50.0 2.4 %inverse_own.1 = (bf16[40,2,128,256]{3,2,1,0:T(8,128)(2,1)}, bf16[6,2,128,256]{3,2,1,0:T(8,128)(2,1)S(1)}) custom-call(f32[20,64,128]{2,1,0:T(8,128)S(1)} %bitcast.11, bf16[40,2,128,256]{3,2,1,0:T(8,128)(2,1)S(1)} %bitcast.8, bf16[128,192]{1,0:T(8,128)(2,1)S(1)} %get-tuple-element.33.rows_ref, bf16[256,256]{1,0:T(8,128)(2,1)S(1)} %get-tuple-element.34.even_ref, ...), custom_call_target="tpu_custom_call" | custom-call | flops 671088640 | bytes 5898240 | tf_op jit(solution)/shard_map/inverse_own/pallas_call | solution.py:368
  52.4 0.0 collective-permute-done.2.modes_ref
  52.4 2.6 %inverse_other.1 = bf16[40,2,128,256]{3,2,1,0:T(8,128)(2,1)} custom-call(f32[20,64,128]{2,1,0:T(8,128)S(1)} %collective-permute-done.2.modes_ref, bf16[40,2,128,256]{3,2,1,0:T(8,128)(2,1)S(1)} %bitcast.9, bf16[128,192]{1,0:T(8,128)(2,1)S(1)} %get-tuple-element.33.rows_ref, ...), custom_call_target="tpu_custom_call", output_to_operand_aliasing={{}: (9, {})} | custom-call | flops 671088640 | bytes 5898240 | tf_op jit(solution)/shard_map/inverse_other/pallas_call | solution.py:368
  (5 shorter events, 0.1 us)
Async XLA Ops:
  0.0 4.8 %copy-start.2 = (s32[2]{0:T(128)S(1)}, s32[2]{0:T(128)}, u32[]{:S(2)}) copy-start(s32[2]{0:T(128)} %param.7) | copy-start | bytes 28
  0.0 4.8 %copy-start.3 = (s32[16]{0:T(128)S(1)}, s32[16]{0:T(128)}, u32[]{:S(2)}) copy-start(s32[16]{0:T(128)} %param.8) | copy-start | bytes 196
  0.0 4.9 %copy-start.1 = (f32[5]{0:T(128)S(1)}, f32[5]{0:T(128)}, u32[]{:S(2)}) copy-start(f32[5]{0:T(128)} %param.9) | copy-start | bytes 64
  3.3 3.8 %collective-permute-start = (f32[20,64,128]{2,1,0:T(8,128)S(1)}, f32[20,64,128]{2,1,0:T(8,128)S(1)}, u32[]{:S(2)}, u32[]{:S(2)}) collective-permute-start(f32[20,64,128]{2,1,0:T(8,128)S(1)} %get-tuple-element.25), channel_id=1, source_target_pairs={{0,16},{16,0},{32,48},{48,32},{64,80},{80,64},{96,112},{112,96},{1... | collective-permute-start | bytes 1966088 | tf_op jit(solution)/shard_map/ppermute | solution.py:425
  7.2 22.7 %copy-start = (f32[5,16,64,64]{3,2,1,0:T(8,128)S(1)}, f32[5,16,64,64]{3,2,1,0:T(8,128)}, u32[]{:S(2)}) copy-start(f32[5,16,64,64]{3,2,1,0:T(8,128)} %param.6) | copy-start | bytes 3932164
  28.0 4.1 %collective-permute-start.1 = (f32[40,128]{1,0:T(8,128)S(1)}, f32[40,128]{1,0:T(8,128)S(1)}, u32[]{:S(2)}, u32[]{:S(2)}) collective-permute-start(f32[40,128]{1,0:T(8,128)S(1)} %sum_pieces.1.after_ref), channel_id=1, source_target_pairs={{0,3},{1,2},{2,1},{3,0},{4,7},{5,6},{6,5},{7,4},{8,11},{9,10},{10,... | collective-permute-start | bytes 61448 | tf_op jit(solution)/shard_map/ppermute | solution.py:433
  29.9 20.1 %slice-start = ((s8[5242880]{0:T(1024)(128)(4,1)}), s8[4194304]{0:T(1024)(128)(4,1)S(1)}, s32[]{:S(2)}) async-start(s8[5242880]{0:T(1024)(128)(4,1)} %bitcast.6), calls=%async_computation.2 | async-start | bytes 8388608
  29.9 20.1 %slice-start.1 = ((s8[5242880]{0:T(1024)(128)(4,1)}), s8[1048576]{0:T(1024)(128)(4,1)S(1)}, s32[]{:S(2)}) async-start(s8[5242880]{0:T(1024)(128)(4,1)} %bitcast.6), calls=%async_computation.3 | async-start | bytes 2097152
  45.9 6.5 %collective-permute-start.2 = (f32[20,64,128]{2,1,0:T(8,128)S(1)}, f32[20,64,128]{2,1,0:T(8,128)S(1)}, u32[]{:S(2)}, u32[]{:S(2)}) collective-permute-start(f32[20,64,128]{2,1,0:T(8,128)S(1)} %bitcast.10), channel_id=1, source_target_pairs={{0,16},{16,0},{32,48},{48,32},{64,80},{80,64},{96,112},{112,96},{1... | collective-permute-start | bytes 1966088 | tf_op jit(solution)/shard_map/ppermute | solution.py:440
